TPU v7x, 512 devices: a whole 4x8x8 slice. The times are simulated.
512 devices in a mesh: ctx: 32 (over z, x), head: 8 (over y_hi, core), dp: 2 (over y_lo).
Axes of the slice: x: 4, y: 8 (y_hi: 4, y_lo: 2; y = y_hi * 2 + y_lo), z: 8, core: 2. Of those that a mesh axis runs over, the one named last changes fastest.
Arguments:
- latents: bfloat16 [2, 4096, 512], P('dp', 'ctx'), may hold values from -6 to 6
- k_rope: bfloat16 [2, 4096, 64], P('dp', 'ctx'), may hold values from -3 to 3
- q_nope: bfloat16 [2, 4096, 2048], P('dp', 'ctx', 'head'), may hold values from -6 to 6
- q_rope: bfloat16 [2, 4096, 1024], P('dp', 'ctx', 'head')
- grad_out: bfloat16 [2, 4096, 2048], P('dp', 'ctx', 'head'), may hold values from -6 to 6
- saved_out: bfloat16 [2, 4096, 2048], P('dp', 'ctx', 'head'), may hold values from -6 to 6
- w_key: bfloat16 [512, 2048], P(None, 'head'), may hold values from -0.25 to 0.25
- w_value: bfloat16 [512, 2048], P(None, 'head'), may hold values from -0.25 to 0.25
- group_order: int32 [64], replicated, may hold values from 0 to 63, each once
Outputs:
- grad_q_nope: bfloat16 [2, 4096, 2048], P('dp', 'ctx', 'head')
- grad_q_rope: bfloat16 [2, 4096, 1024], P('dp', 'ctx', 'head')
- grad_latents: bfloat16 [2, 4096, 512], P('dp', 'ctx')
- grad_k_rope: bfloat16 [2, 4096, 64], P('dp', 'ctx')
- grad_w_key: float32 [512, 2048], P(('ctx', 'dp'), 'head')
- grad_w_value: float32 [512, 2048], P(('ctx', 'dp'), 'head')
Inputs may be any that keep to these rules, and one draw needn't show every extreme that they name: `group_order`: every block number appears once.
All inputs are finite; a program needn't handle non-finite values.
Results may differ from a plain program's by a relative error of at most 0.0095.
Values may be sent and summed in bfloat16 or wider, within the bound.
A program may use at most 64 MiB of HBM per device.

v0:
```python
import jax
import jax.numpy as jnp
from jax import lax
from jax.sharding import PartitionSpec as P

DN = 128
DR = 64
DV = 128
TOK_DEV = 128


neg_big = -1e30
block_rows = 512


def group_positions(group_order, first_row, row_total, half_group):
    row_ids = first_row + jnp.arange(row_total, dtype=jnp.int32)
    group_index = row_ids // half_group
    group_ids = jnp.arange(group_order.shape[0], dtype=jnp.int32)
    group_of = jnp.sum(
        jnp.where(group_index[:, None] == group_ids[None, :], group_order[None, :], 0), axis=1
    )
    return group_of * half_group + row_ids % half_group


def fold_blocks(block_step, running, pieces):
    row_total = pieces[0].shape[1]
    block_count = row_total // block_rows
    stacked = tuple(
        (
            jnp.swapaxes(
                piece_arr.reshape(
                    (piece_arr.shape[0], block_count, block_rows) + piece_arr.shape[2:]
                ),
                0,
                1,
            )
            for piece_arr in pieces
        )
    )

    def visit_block(state_now, scan_item):
        step_index, blocks = scan_item
        return (block_step(state_now, blocks, step_index * block_rows), None)

    running, ignored = lax.scan(
        visit_block, running, (jnp.arange(block_count, dtype=jnp.int32), stacked)
    )
    return running


def attend_scores(query_nope, query_rope, key_nope, key_rope, query_pos, key_pos, score_scale):
    raw_scores = jnp.einsum(
        "qhd,khd->hqk", query_nope, key_nope, preferred_element_type=jnp.float32
    )
    raw_scores = raw_scores + jnp.einsum(
        "qhd,kd->hqk", query_rope, key_rope, preferred_element_type=jnp.float32
    )
    visible = key_pos[None, None, :] <= query_pos[None, :, None]
    return (raw_scores * score_scale, visible)


def shards(latents, k_rope, q_nope, q_rope, grad_out, saved_out, w_key, w_value, group_order):
    tokens = latents.shape[1]
    head_count = q_nope.shape[2] // DN
    half_group = TOK_DEV // 2
    score_scale = (DN + DR) ** (-0.5)
    my_index = lax.axis_index("ctx")
    my_pos = group_positions(group_order, my_index * tokens, tokens, half_group)
    query_nope = q_nope[0].reshape(tokens, head_count, DN)
    query_rope = q_rope[0].reshape(tokens, head_count, DR)
    upstream = grad_out[0].reshape(tokens, head_count, DV)
    saved_rows = saved_out[0].reshape(tokens, head_count, DV)
    row_delta = jnp.sum(upstream.astype(jnp.float32) * saved_rows.astype(jnp.float32), axis=2).T
    own_key = jnp.dot(latents[0], w_key, preferred_element_type=jnp.float32).astype(jnp.bfloat16)
    own_value = jnp.dot(latents[0], w_value, preferred_element_type=jnp.float32).astype(
        jnp.bfloat16
    )
    own_keys = own_key.reshape(tokens, head_count, DN)
    own_values = own_value.reshape(tokens, head_count, DV)
    own_rope = k_rope[0]

    def unpack(blocks):
        block_count = blocks[0].shape[1]
        key_block = jnp.dot(blocks[0][0], w_key, preferred_element_type=jnp.float32).astype(
            jnp.bfloat16
        )
        value_block = jnp.dot(blocks[0][0], w_value, preferred_element_type=jnp.float32).astype(
            jnp.bfloat16
        )
        return (
            key_block.reshape(block_count, head_count, DN),
            value_block.reshape(block_count, head_count, DV),
            blocks[1][0],
        )

    def over_keys(block_step, initial):
        return fold_blocks(
            block_step,
            initial,
            (
                lax.all_gather(latents, "ctx", axis=1, tiled=True),
                lax.all_gather(k_rope, "ctx", axis=1, tiled=True),
            ),
        )

    def stats_step(running, blocks, start_row):
        row_top, row_total = running
        key_block, ignored, rope_block = unpack(blocks)
        key_pos = group_positions(group_order, start_row, key_block.shape[0], half_group)
        scores, visible = attend_scores(
            query_nope, query_rope, key_block, rope_block, my_pos, key_pos, score_scale
        )
        block_top = jnp.max(jnp.where(visible, scores, neg_big), axis=2)
        new_top = jnp.maximum(row_top, block_top)
        exp_rows = jnp.where(visible, jnp.exp(scores - new_top[:, :, None]), 0.0)
        return (new_top, row_total * jnp.exp(row_top - new_top) + jnp.sum(exp_rows, axis=2))

    start_top = jnp.full((head_count, tokens), neg_big, jnp.float32)
    row_top, row_total = over_keys(
        stats_step, (start_top, jnp.zeros((head_count, tokens), jnp.float32))
    )
    log_total = row_top + jnp.log(row_total)

    def query_grad_step(running, blocks, start_row):
        grad_nope, grad_rope = running
        key_block, value_block, rope_block = unpack(blocks)
        key_pos = group_positions(group_order, start_row, key_block.shape[0], half_group)
        scores, visible = attend_scores(
            query_nope, query_rope, key_block, rope_block, my_pos, key_pos, score_scale
        )
        prob_rows = jnp.where(visible, jnp.exp(scores - log_total[:, :, None]), 0.0)
        dprob_rows = jnp.einsum(
            "qhd,khd->hqk", upstream, value_block, preferred_element_type=jnp.float32
        )
        dscore_rows = (prob_rows * (dprob_rows - row_delta[:, :, None]) * score_scale).astype(
            jnp.bfloat16
        )
        grad_nope = grad_nope + jnp.einsum(
            "hqk,khd->qhd", dscore_rows, key_block, preferred_element_type=jnp.float32
        )
        grad_rope = grad_rope + jnp.einsum(
            "hqk,kd->qhd", dscore_rows, rope_block, preferred_element_type=jnp.float32
        )
        return (grad_nope, grad_rope)

    grad_nope, grad_rope = over_keys(
        query_grad_step,
        (
            jnp.zeros((tokens, head_count, DN), jnp.float32),
            jnp.zeros((tokens, head_count, DR), jnp.float32),
        ),
    )
    all_lse, all_delta = (
        lax.all_gather(log_total.T[None], "ctx", axis=1, tiled=True),
        lax.all_gather(row_delta.T[None], "ctx", axis=1, tiled=True),
    )

    def key_grad_step(running, blocks, start_row):
        grad_key, grad_krope, grad_value = running
        block_count = blocks[0].shape[1]
        far_nope = blocks[0][0].reshape(block_count, head_count, DN)
        far_rope = blocks[1][0].reshape(block_count, head_count, DR)
        far_upstream = blocks[2][0].reshape(block_count, head_count, DV)
        far_lse = lax.dynamic_slice_in_dim(all_lse[0], start_row, block_count, 0).T
        far_delta = lax.dynamic_slice_in_dim(all_delta[0], start_row, block_count, 0).T
        query_pos = group_positions(group_order, start_row, block_count, half_group)
        scores, visible = attend_scores(
            far_nope, far_rope, own_keys, own_rope, query_pos, my_pos, score_scale
        )
        prob_rows = jnp.where(visible, jnp.exp(scores - far_lse[:, :, None]), 0.0)
        dprob_rows = jnp.einsum(
            "qhd,khd->hqk", far_upstream, own_values, preferred_element_type=jnp.float32
        )
        dscore_rows = (prob_rows * (dprob_rows - far_delta[:, :, None]) * score_scale).astype(
            jnp.bfloat16
        )
        grad_key = grad_key + jnp.einsum(
            "hqk,qhd->khd", dscore_rows, far_nope, preferred_element_type=jnp.float32
        )
        grad_krope = grad_krope + jnp.einsum(
            "hqk,qhd->kd", dscore_rows, far_rope, preferred_element_type=jnp.float32
        )
        grad_value = grad_value + jnp.einsum(
            "hqk,qhd->khd",
            prob_rows.astype(jnp.bfloat16),
            far_upstream,
            preferred_element_type=jnp.float32,
        )
        return (grad_key, grad_krope, grad_value)

    initial = (
        jnp.zeros((tokens, head_count, DN), jnp.float32),
        jnp.zeros((tokens, DR), jnp.float32),
        jnp.zeros((tokens, head_count, DV), jnp.float32),
    )
    grad_key, grad_krope, grad_value = fold_blocks(
        key_grad_step,
        initial,
        (
            lax.all_gather(q_nope, "ctx", axis=1, tiled=True),
            lax.all_gather(q_rope, "ctx", axis=1, tiled=True),
            lax.all_gather(grad_out, "ctx", axis=1, tiled=True),
        ),
    )
    key_flat = grad_key.astype(jnp.bfloat16).reshape(tokens, head_count * DN)
    value_flat = grad_value.astype(jnp.bfloat16).reshape(tokens, head_count * DV)
    paired_grads = jnp.concatenate((key_flat, value_flat), axis=1)
    projections = jnp.concatenate((w_key, w_value), axis=1)
    partial_latent = jnp.einsum(
        "kc,lc->kl", paired_grads, projections, preferred_element_type=jnp.float32
    )
    total_latent, total_krope = lax.psum((partial_latent, grad_krope), "head")
    latent_part = latents[0]
    summed = lax.psum_scatter(
        jnp.einsum("kl,kc->lc", latent_part, paired_grads, preferred_element_type=jnp.float32),
        ("ctx", "dp"),
        scatter_dimension=0,
        tiled=True,
    )
    key_width = head_count * DN
    return (
        grad_nope.astype(jnp.bfloat16).reshape(1, tokens, head_count * DN),
        grad_rope.astype(jnp.bfloat16).reshape(1, tokens, head_count * DR),
        total_latent.astype(jnp.bfloat16)[None],
        total_krope.astype(jnp.bfloat16)[None],
        summed[:, :key_width],
        summed[:, key_width:],
    )


def solution(mesh):
    return jax.shard_map(
        shards,
        mesh=mesh,
        in_specs=(
            P("dp", "ctx", None),
            P("dp", "ctx", None),
            P("dp", "ctx", "head"),
            P("dp", "ctx", "head"),
            P("dp", "ctx", "head"),
            P("dp", "ctx", "head"),
            P(None, "head"),
            P(None, "head"),
            P(),
        ),
        out_specs=(
            P("dp", "ctx", "head"),
            P("dp", "ctx", "head"),
            P("dp", "ctx", None),
            P("dp", "ctx", None),
            P(("ctx", "dp"), "head"),
            P(("ctx", "dp"), "head"),
        ),
        check_vma=False,
    )
```

profile of v0, /device:TPU:16, one launch (start us, length us, event | category | flops | bytes accessed | tf_op | source)
XLA Modules:
  0.0 730.7 jit_solution(381701000340493602)
XLA Ops:
  13.8 56.5 %all_gather.24 = bf16[1,4096,64]{1,2,0:T(8,128)(2,1)S(1)} all-gather(bf16[1,128,64]{1,2,0:T(8,128)(2,1)} %param.16), channel_id=1, replica_groups=mesh['ctx'=32,'head'=8,'dp'=2] {'ctx'}, dimensions={1}, use_global_device_ids=true | all-gather | bytes 540672 | tf_op jit(solution)/shard_map/all_gather | solution.py:103
  73.9 42.1 %all-gather.1 = f32[4096,2]{0,1:T(2,128)S(1)} all-gather(f32[128,2]{0,1:T(2,128)S(1)} %fusion.64), channel_id=3, replica_groups=mesh['ctx'=32,'head'=8,'dp'=2] {'ctx'}, dimensions={0}, use_global_device_ids=true | all-gather | bytes 33792 | tf_op jit(solution)/shard_map/all_gather | solution.py:156
  116.1 35.1 %while.47 = (s32[]{:T(128)}, f32[2,128]{1,0:T(2,128)S(1)}, f32[2,128]{1,0:T(2,128)S(1)}, s32[8]{0:T(128)S(1)}, s32[64]{0:T(128)}, /*index=5*/s32[128]{0:T(128)S(...) while((s32[]{:T(128)}, f32[2,128]{1,0:T(2,128)S(1)}, ...), condition=%wide.region_5.6_spmd.clone, body=%wide.region_1.5_spmd.clone.sunk | while | flops 185777920 | bytes 3794880 | solution.py:46
  118.3 1.5 convolution_convert_fusion.8
  122.6 1.5 convolution_convert_fusion.8
  127.0 1.5 convolution_convert_fusion.8
  131.4 1.5 convolution_convert_fusion.8
  135.8 1.5 convolution_convert_fusion.8
  140.2 1.5 convolution_convert_fusion.8
  144.6 1.5 convolution_convert_fusion.8
  149.0 1.5 convolution_convert_fusion.8
  151.2 40.6 %all-gather = f32[4096,2]{0,1:T(2,128)S(1)} all-gather(f32[128,2]{0,1:T(2,128)S(1)} %bitcast.309), channel_id=2, replica_groups=mesh['ctx'=32,'head'=8,'dp'=2] {'ctx'}, dimensions={0}, use_global_device_ids=true | all-gather | bytes 33792 | tf_op jit(solution)/shard_map/all_gather | solution.py:155
  191.8 78.7 %all-gather.9.cloned.1.call-done = bf16[1,4096,256]{2,1,0:T(8,128)(2,1)} async-done(((bf16[1,128,256]{2,1,0:T(8,128)(2,1)}), bf16[1,4096,256]{2,1,0:T(8,128)(2,1)}) %all-gather.9.cloned.1.call-update) | async-done | bytes 2097168 | tf_op jit(solution)/shard_map/all_gather | solution.py:201
  270.4 83.9 %all-gather.13.cloned.1.call-done = bf16[1,4096,256]{2,1,0:T(8,128)(2,1)} async-done(((bf16[1,128,256]{2,1,0:T(8,128)(2,1)}), bf16[1,4096,256]{2,1,0:T(8,128)(2,1)}) %all-gather.13.cloned.1.call-update) | async-done | bytes 2097168 | tf_op jit(solution)/shard_map/all_gather | solution.py:203
  354.3 49.8 %while.49 = (s32[]{:T(128)}, f32[128,2,128]{0,2,1:T(8,128)S(1)}, f32[128,64]{0,1:T(8,128)S(1)}, f32[128,2,128]{0,2,1:T(8,128)S(1)}, bf16[8,1,512,256]{3,2,0,1:T(...) while((s32[]{:T(128)}, f32[128,2,128]{0,2,1:T(8,128)S(1)}, ...), condition=%wide.region_12.13_spmd.clone, body=%wide.region_10.12_spmd.clone.sunk | while | flops 169277952 | bytes 8246287 | solution.py:46
  405.9 45.3 %while.48 = (s32[]{:T(128)}, f32[128,2,128]{0,2,1:T(8,128)S(1)}, f32[128,2,64]{0,2,1:T(8,128)S(1)}, bf16[8,1,512,512]{3,2,1,0:T(8,128)(2,1)}, bf16[512,256]{1,0:...) while((s32[]{:T(128)}, f32[128,2,128]{0,2,1:T(8,128)S(1)}, ...), condition=%wide.region_9.10_spmd.clone, body=%wide.region_7.9_spmd.clone.sunk | while | flops 404240896 | bytes 6601704 | solution.py:46
  405.9 1.4 convolution_convert_fusion.9
  409.4 1.4 convolution_convert_fusion.10
  411.6 1.4 convolution_convert_fusion.9
  415.1 1.4 convolution_convert_fusion.10
  417.2 1.4 convolution_convert_fusion.9
  420.7 1.4 convolution_convert_fusion.10
  422.9 1.4 convolution_convert_fusion.9
  426.4 1.4 convolution_convert_fusion.10
  428.5 1.4 convolution_convert_fusion.9
  432.1 1.4 convolution_convert_fusion.10
  434.2 1.4 convolution_convert_fusion.9
  437.7 1.4 convolution_convert_fusion.10
  443.4 1.4 convolution_convert_fusion.10
  445.5 1.4 convolution_convert_fusion.9
  453.0 31.3 %all-reduce.2 = (bf16[128,512]{1,0:T(8,128)(2,1)}, bf16[128,64]{0,1:T(8,128)(2,1)}) all-reduce(f32[128,512]{1,0:T(8,128)S(1)} %fusion.60, f32[128,64]{0,1:T(8,128)S(1)} %get-tuple-element.532), channel_id=1, replica_groups=mesh['ctx'=32,'head'=8,'dp'=2] {'head'}, use_global_device_ids=true, to_apply=%region_13.14 | all-reduce | flops 73728 | bytes 442368 | tf_op jit(solution)/shard_map/psum | solution.py:213
  484.3 238.6 %reduce-scatter.4.cloned.1.call-done = f32[8,512]{1,0:T(8,128)} async-done(((f32[512,512]{1,0:T(8,128)}), f32[8,512]{1,0:T(8,128)}) %reduce-scatter.4.cloned.1.call-update) | async-done | bytes 16400
  (363 shorter events, 96.1 us)
Async XLA Ops:
  7.2 108.9 %all-gather.7.cloned.1.call-start = ((), (), s32[]{:S(2)}) async-start(), calls=%async_computation.1 | async-start | bytes 4325376 | tf_op jit(solution)/shard_map/all_gather | solution.py:102
  7.9 183.9 %all-gather.11.cloned.1.call-start = ((), (), s32[]{:S(2)}) async-start(), calls=%async_computation.3 | async-start | bytes 1081344 | tf_op jit(solution)/shard_map/all_gather | solution.py:202
  8.6 261.8 %all-gather.9.cloned.1.call-start = ((), (), s32[]{:S(2)}) async-start(), calls=%async_computation.2 | async-start | bytes 2162688 | tf_op jit(solution)/shard_map/all_gather | solution.py:201
  9.4 344.9 %all-gather.13.cloned.1.call-start = ((), (), s32[]{:S(2)}) async-start(), calls=%async_computation.4 | async-start | bytes 2162688 | tf_op jit(solution)/shard_map/all_gather | solution.py:203
  10.0 712.9 %reduce-scatter.4.cloned.1.call-start = ((), (), s32[]{:S(2)}) async-start(), calls=%async_computation.5 | async-start | bytes 1064960
  116.1 238.3 %copy-start.3 = (bf16[1,128,64]{1,2,0:T(8,128)(2,1)S(1)}, bf16[1,128,64]{1,2,0:T(8,128)(2,1)}, u32[]{:S(2)}) copy-start(bf16[1,128,64]{1,2,0:T(8,128)(2,1)} %param.16) | copy-start | bytes 49156
  354.3 49.9 %copy-start.2 = (bf16[1,128,512]{2,1,0:T(8,128)(2,1)S(1)}, bf16[1,128,512]{2,1,0:T(8,128)(2,1)}, u32[]{:S(2)}) copy-start(bf16[1,128,512]{2,1,0:T(8,128)(2,1)} %param.15) | copy-start | bytes 393220
  404.1 1.7 copy-start
  404.2 1.7 copy-start.1
  404.2 1.7 copy-start.4
Sparse Core Ops, SparseCore 0:
  11.2 93.0 all-gather.6
  107.4 78.4 all-gather.10
  189.1 81.2 all-gather.8
  273.4 80.8 all-gather.12
  406.0 316.8 reduce-scatter.3
where the time goes:
time: 733 us; the launch traced here: 731 us
  waiting for transfers between devices  404 us (55%)
  blocking collectives  170 us (23%)
  matrix products  64.3 us (9%)
  local copies, waits for them, and re-layouts  41.5 us (6%)
  other arithmetic  18.7 us (3%)
  loops' own time  17.8 us (2%)
  between operations  14.1 us (2%)
    unnamed x6, waiting for transfers between devices  241 us
    all_gather x1, waiting for transfers between devices, shards(): lax.all_gather(grad_out, 'ctx', axis=1, tiled=True)  83.9 us
    all_gather x1, waiting for transfers between devices, shards(): lax.all_gather(q_nope, 'ctx', axis=1, tiled=True)  78.7 us
    all_gather x1, blocking collectives, over_keys(): lax.all_gather(k_rope, 'ctx', axis=1, tiled=True)  56.5 us
    all_gather x1, blocking collectives, shards(): lax.all_gather(row_delta.T[None], 'ctx', axis=1, tiled=True)  42.1 us
    all_gather x1, blocking collectives, shards(): lax.all_gather(log_total.T[None], 'ctx', axis=1, tiled=True)  40.6 us
    dynamic_slice x64, local copies, waits for them, and re-layouts, fold_blocks(): lax.scan(visit_block, running, (jnp.arange(block_count, dtype=jnp.int32),...  33.2 us
    psum x1, blocking collectives, shards(): total_latent, total_krope = lax.psum((partial_latent, grad_krope), 'head')  31.3 us
  transfers between devices with their start and end apart: 5, of which 3 were waited for; matrix products, arithmetic and copies ran while one was open for 11% of the time, Pallas kernels for 0%

commit v1 on v0

v1 whole, which is shorter than its diff:
```python
import functools
import math

import jax
import jax.numpy as jnp
from jax import lax
from jax.experimental import pallas as pl
from jax.experimental.pallas import tpu as pltpu
from jax.sharding import PartitionSpec as P

DL = 512
DN = 128
DR = 64
DV = 128
NX = 4
CORES = 2
HALF_GROUP = 64

MESH = pl.DeviceIdType.MESH
MASKED = -1.5e38
FLOOR = -1.0e38
F32 = jnp.float32
BF16 = jnp.bfloat16

NT = (((1,), (1,)), ((), ()))


def dot(a, b):
    return jnp.dot(a, b, preferred_element_type=F32)


def dot_nt(a, b):
    return lax.dot_general(a, b, NT, preferred_element_type=F32)


def ring_offset(r, n):
    odd = lax.rem(r, 2)
    return odd * lax.div(r + 1, 2) + (1 - odd) * (n - lax.div(r, 2))


def kernel(
    nz, nyh, tok,
    lat_in, kr_in, qn_in, qr_in, go_in, so_in, wk_in, wv_in, order,
    gqn_out, gqr_out, gl_out, gkr_out, gwk_out, gwv_out,
    lat, krs, q, saved, w, delta, qpos, qcat, qgo, latt, keyst,
    pexp, dsx, mscr, lscr, stats, dsall, gall,
    glsend, glsib, glz, glzr, tot, ychunk, yrecv, final,
    gqf, gqb, gqr, gwf, gwb, gwr, gwzf, gwzb, gwzr, gwdf, gwdr,
    local_sem, lat_s, lat_r, fwd_s, fwd_r, q_s, q_r, de_s, de_r, st_s, st_r,
    sib_s, sib_r, glz_s, glz_r, gq_s, gq_r, gwx_s, gwx_r, gwz_s, gwz_r,
    y_s, y_r, fin_s, fin_r, dp_s, dp_r,
):
    ctx = lax.axis_index("ctx")
    head = lax.axis_index("head")
    dp = lax.axis_index("dp")
    z, x = lax.div(ctx, NX), lax.rem(ctx, NX)
    y, core = lax.div(head, CORES), lax.rem(head, CORES)
    heads = nyh * CORES
    half = tok // CORES
    queries = NX * tok
    keys = nz * tok
    score_scale = (DN + DR) ** -0.5
    log2_scale = score_scale * math.log2(math.e)

    def at_z(z_peer):
        return {"ctx": z_peer * NX + x, "head": head, "dp": dp}

    def at_x(x_peer):
        return {"ctx": z * NX + x_peer, "head": head, "dp": dp}

    def at_head(peer):
        return {"ctx": ctx, "head": peer, "dp": dp}

    sibling = at_head(y * CORES + (1 - core))
    other_dp = {"ctx": ctx, "head": head, "dp": 1 - dp}

    def remote(src, dst, send, recv, device):
        return pltpu.make_async_remote_copy(
            src_ref=src, dst_ref=dst, send_sem=send, recv_sem=recv,
            device_id=device, device_id_type=MESH,
        )

    z_peers = [lax.rem(z + (k if k <= nz // 2 else k), nz) for k in range(1, nz)]
    x_peers = [lax.rem(x + k, NX) for k in range(1, NX)]
    y_peers = [lax.rem(y + k, nyh) for k in range(1, nyh)]
    head_peers = [lax.rem(head + k, heads) for k in range(1, heads)]

    def z_at(r):
        return lax.rem(z + ring_offset(r, nz), nz)

    local = [
        pltpu.make_async_copy(lat_in.at[0], lat.at[z, :, pl.ds(0, DL)], local_sem.at[0]),
        pltpu.make_async_copy(kr_in.at[0], krs, local_sem.at[1]),
        pltpu.make_async_copy(qn_in.at[0], q.at[x, :, pl.ds(0, 2 * DN)], local_sem.at[2]),
        pltpu.make_async_copy(qr_in.at[0], q.at[x, :, pl.ds(2 * DN, 2 * DR)], local_sem.at[3]),
        pltpu.make_async_copy(
            go_in.at[0], q.at[x, :, pl.ds(2 * DN + 2 * DR, 2 * DV)], local_sem.at[4]
        ),
        pltpu.make_async_copy(so_in.at[0], saved, local_sem.at[5]),
        pltpu.make_async_copy(wk_in, w.at[:, pl.ds(0, 2 * DN)], local_sem.at[6]),
        pltpu.make_async_copy(wv_in, w.at[:, pl.ds(2 * DN, 2 * DV)], local_sem.at[7]),
    ]
    for copy in local:
        copy.start()

    barrier = pltpu.get_barrier_semaphore()
    targets = (
        [at_z(p) for p in z_peers] + [at_x(p) for p in x_peers]
        + [at_head(p) for p in head_peers] + [other_dp]
    )
    for target in targets:
        pl.semaphore_signal(barrier, inc=1, device_id=target, device_id_type=MESH)
    for copy in local:
        copy.wait()
    rope_lanes = jnp.concatenate([krs[...], jnp.zeros((tok, DR), BF16)], axis=1)
    lat[z, :, DL:] = rope_lanes
    pl.semaphore_wait(barrier, len(targets))

    own_rows = pl.ds(pl.multiple_of(core * half, half), half)
    other_rows = pl.ds(pl.multiple_of((1 - core) * half, half), half)

    def lat_copy(k, src_z, dst_z):
        return remote(
            lat.at[src_z, own_rows], lat.at[src_z, own_rows], lat_s.at[k], lat_r.at[src_z],
            at_z(dst_z),
        )

    def forward_copy(src_z):
        return remote(
            lat.at[src_z, own_rows], lat.at[src_z, own_rows], fwd_s.at[src_z], fwd_r.at[src_z],
            sibling,
        )

    def forward_arrival(src_z):
        return remote(
            lat.at[src_z, other_rows], lat.at[src_z, other_rows], fwd_s.at[src_z],
            fwd_r.at[src_z], sibling,
        )

    q_copies = [
        remote(q.at[x], q.at[x], q_s.at[k], q_r.at[x], at_x(p)) for k, p in enumerate(x_peers)
    ]
    lat_copies = [lat_copy(r - 1, z, z_at(r)) for r in range(1, nz)]
    for k in range(max(len(q_copies), len(lat_copies))):
        if k < len(q_copies):
            q_copies[k].start()
        if k < len(lat_copies):
            lat_copies[k].start()

    upstream = q[x, :, 2 * DN + 2 * DR:].astype(F32)
    product = (upstream * saved[...].astype(F32)).T
    delta[x, 0:1, :] = jnp.sum(product[:DV], axis=0, keepdims=True)
    delta[x, 1:2, :] = jnp.sum(product[DV:], axis=0, keepdims=True)
    delta_copies = [
        remote(delta.at[x], delta.at[x], de_s.at[k], de_r.at[x], at_x(p))
        for k, p in enumerate(x_peers)
    ]
    for copy in delta_copies:
        copy.start()

    lane = lax.broadcasted_iota(jnp.int32, (1, tok), 1)
    for p in range(NX):
        first = 2 * (z * NX + p)
        qpos[0:1, p * tok:(p + 1) * tok] = jnp.where(
            lane < HALF_GROUP,
            order[first] * HALF_GROUP + lane,
            order[first + 1] * HALF_GROUP + lane - HALF_GROUP,
        )

    for p in x_peers:
        remote(q.at[p], q.at[p], q_s.at[0], q_r.at[p], at_x(p)).wait_recv()
        remote(delta.at[p], delta.at[p], de_s.at[0], de_r.at[p], at_x(p)).wait_recv()
    for p in range(NX):
        rows = pl.ds(p * tok, tok)
        for h in range(2):
            qcat[h, rows, 0:DN] = q[p, :, h * DN:(h + 1) * DN]
            qcat[h, rows, DN:] = q[p, :, 2 * DN:2 * DN + 2 * DR]
            qgo[h, rows, :] = q[p, :, 2 * DN + 2 * DR + h * DV:2 * DN + 2 * DR + (h + 1) * DV]

    def first_pass(r, carry):
        block = z_at(r)

        @pl.when(r < nz - 1)
        def _():
            coming = z_at(r + 1)
            lat_copy(0, coming, coming).wait_recv()
            forward_copy(coming).start()

        @pl.when(r > 0)
        def _():
            forward_arrival(block).wait_recv()

        latents = lat[block, :, 0:DL]
        rope0 = lat[block, :, DL:]
        rope1 = jnp.concatenate([rope0[:, DR:], rope0[:, :DR]], axis=1)
        projected = dot(latents, w[...]).astype(BF16)
        columns = pl.ds(pl.multiple_of(r * tok, tok), tok)
        latt[:, columns] = latents.T
        first = 2 * (block * NX + x)
        row = lax.broadcasted_iota(jnp.int32, (HALF_GROUP, queries), 0)
        where_q = qpos[0:1, :]
        seen = jnp.concatenate(
            [row <= where_q - order[first + g] * HALF_GROUP for g in range(2)], axis=0
        )
        for h in range(2):
            key = jnp.concatenate(
                [projected[:, h * DN:(h + 1) * DN], rope0 if h == 0 else rope1], axis=1
            )
            keyst[h, :, columns] = key.T
            scores = jnp.where(seen, dot_nt(key, qcat[h]) * log2_scale, MASKED)
            top = jnp.maximum(jnp.max(scores, axis=0, keepdims=True), FLOOR)
            weight = jnp.exp2(scores - top)
            mscr[h, r] = top
            lscr[h, r] = jnp.sum(weight, axis=0, keepdims=True)
            dprobs = dot_nt(projected[:, 2 * DN + h * DV:2 * DN + (h + 1) * DV], qgo[h])
            row_delta = jnp.concatenate([delta[p, h:h + 1, :] for p in range(NX)], axis=1)
            pexp[h, r] = weight
            dsx[h, r] = weight * (dprobs - row_delta)
        return carry

    lax.fori_loop(0, nz, first_pass, 0)

    for h in range(2):
        top = mscr[h, 0]
        for r in range(1, nz):
            top = jnp.maximum(top, mscr[h, r])
        total = jnp.zeros_like(top)
        for r in range(nz):
            total += lscr[h, r] * jnp.exp2(mscr[h, r] - top)
        stats[x, 2 * h:2 * h + 1, :] = top
        stats[x, 2 * h + 1:2 * h + 2, :] = total
    stat_copies = [
        remote(stats.at[x], stats.at[x], st_s.at[k], st_r.at[x], at_x(p))
        for k, p in enumerate(x_peers)
    ]
    for copy in stat_copies:
        copy.start()
    for p in x_peers:
        remote(stats.at[p], stats.at[p], st_s.at[0], st_r.at[p], at_x(p)).wait_recv()
    log_total = []
    for h in range(2):
        top = stats[0, 2 * h:2 * h + 1, :]
        for p in range(1, NX):
            top = jnp.maximum(top, stats[p, 2 * h:2 * h + 1, :])
        total = jnp.zeros_like(top)
        for p in range(NX):
            total += stats[p, 2 * h + 1:2 * h + 2, :] * jnp.exp2(
                stats[p, 2 * h:2 * h + 1, :] - top
            )
        log_total.append(top + jnp.log2(total))

    def sib_copy(r):
        return remote(glsend.at[r, other_rows], glsib.at[r], sib_s.at[r], sib_r.at[r], sibling)

    def glz_copy(r):
        return remote(glz.at[r], glzr.at[z], glz_s.at[r], glz_r.at[z], at_z(z_at(r)))

    def chip_sum(r):
        sib_copy(r).wait_recv()
        return glsend[r, own_rows, :].astype(F32) + glsib[r].astype(F32)

    def second_pass(step, carry):
        r = nz - 1 - step
        rows = pl.ds(pl.multiple_of(r * tok, tok), tok)
        key_parts, value_parts, rope_parts = [], [], []
        for h in range(2):
            factor = jnp.exp2(mscr[h, r] - carry[h])
            probs = (pexp[h, r] * factor).astype(BF16)
            dscores = (dsx[h, r] * (factor * score_scale)).astype(BF16)
            dsall[h, rows, :] = dscores
            joint = dot(dscores, qcat[h])
            key_parts.append(joint[:, :DN].astype(BF16))
            rope_parts.append(joint[:, DN:])
            value_parts.append(dot(probs, qgo[h]).astype(BF16))
        grads = jnp.concatenate(key_parts + value_parts, axis=1)
        gall[rows, :] = grads
        ropes = jnp.where(
            lax.broadcasted_iota(jnp.int32, (tok, 2 * DR), 1) < DR, rope_parts[0], rope_parts[1]
        )
        glsend[r, :, 0:DL] = dot_nt(grads, w[...]).astype(BF16)
        glsend[r, :, DL:] = ropes.astype(BF16)
        sib_copy(r).start()

        @pl.when(step > 0)
        def _():
            glz[r + 1] = chip_sum(r + 1).astype(BF16)
            glz_copy(r + 1).start()

        return carry

    lax.fori_loop(0, nz, second_pass, tuple(log_total))

    parts = [dot(keyst[h], dsall[h]) for h in range(2)]
    stacked = jnp.concatenate(
        [parts[0][:DN], parts[1][:DN], parts[0][DN:] + parts[1][DN:]], axis=0
    )
    turned = stacked.T
    gqb[...] = turned.astype(BF16).reshape(gqb.shape)
    gqf[...] = turned
    gq_copies = [
        remote(gqb.at[p], gqr.at[x], gq_s.at[k], gq_r.at[x], at_x(p))
        for k, p in enumerate(x_peers)
    ]
    for copy in gq_copies:
        copy.start()

    sub = DL // (nz * NX)
    gwf[...] = dot(latt[...], gall[...]).reshape(gwf.shape)
    for p in range(NX):
        gwb[p] = gwf[:, p].astype(BF16)
    gwx_copies = [
        remote(gwb.at[p], gwr.at[x], gwx_s.at[k], gwx_r.at[x], at_x(p))
        for k, p in enumerate(x_peers)
    ]
    for copy in gwx_copies:
        copy.start()

    total = chip_sum(0)
    for k in range(1, nz):
        p = z_at(k)
        remote(glz.at[0], glzr.at[p], glz_s.at[0], glz_r.at[p], at_z(p)).wait_recv()
        total += glzr[p].astype(F32)
    tot[...] = total.reshape(tot.shape)
    ychunk[...] = total.astype(BF16).reshape(ychunk.shape)
    y_copies = [
        remote(ychunk.at[p], yrecv.at[y], y_s.at[k], y_r.at[y], at_head(p * CORES + core))
        for k, p in enumerate(y_peers)
    ]
    for copy in y_copies:
        copy.start()

    own_tok = pl.ds(pl.multiple_of(x * tok, tok), tok)
    mine = gqf[own_tok, :]
    for p in x_peers:
        remote(gqb.at[0], gqr.at[p], gq_s.at[0], gq_r.at[p], at_x(p)).wait_recv()
        mine += gqr[p].astype(F32)
    gqn_out[0] = mine[:, :2 * DN].astype(BF16)
    gqr_out[0] = mine[:, 2 * DN:].astype(BF16)

    part = gwf[:, x]
    for p in x_peers:
        remote(gwb.at[0], gwr.at[p], gwx_s.at[0], gwx_r.at[p], at_x(p)).wait_recv()
        part += gwr[p].astype(F32)
    gwzf[...] = part
    gwzb[...] = part.astype(BF16)
    gwz_copies = [
        remote(gwzb.at[z_at(r)], gwzr.at[z], gwz_s.at[r - 1], gwz_r.at[z], at_z(z_at(r)))
        for r in range(1, nz)
    ]
    for copy in gwz_copies:
        copy.start()

    mine = tot[y]
    for p in y_peers:
        remote(
            ychunk.at[0], yrecv.at[p], y_s.at[0], y_r.at[p], at_head(p * CORES + core)
        ).wait_recv()
        mine += yrecv[p].astype(F32)
    folded = mine[:, DL:] + jnp.concatenate([mine[:, DL + DR:], mine[:, DL:DL + DR]], axis=1)
    slot = core * nyh + y
    final[slot, :, 0:DL] = mine[:, :DL].astype(BF16)
    final[slot, :, DL:] = folded.astype(BF16)
    fin_copies = [
        remote(final.at[slot], final.at[slot], fin_s.at[k], fin_r.at[slot], at_head(p))
        for k, p in enumerate(head_peers)
    ]
    for copy in fin_copies:
        copy.start()

    part = gwzf[z]
    for r in range(1, nz):
        p = z_at(r)
        remote(gwzb.at[0], gwzr.at[p], gwz_s.at[0], gwz_r.at[p], at_z(p)).wait_recv()
        part += gwzr[p].astype(F32)
    gwdf[...] = part.reshape(gwdf.shape)
    dp_copy = remote(gwdf.at[1 - dp], gwdr, dp_s.at[0], dp_r.at[0], other_dp)
    dp_copy.start()

    for p in head_peers:
        from_slot = lax.rem(p, CORES) * nyh + lax.div(p, CORES)
        remote(
            final.at[from_slot], final.at[from_slot], fin_s.at[0], fin_r.at[from_slot], at_head(p)
        ).wait_recv()
    rows_16 = half // nyh
    for k in range(heads):
        gl_out[0, k * rows_16:(k + 1) * rows_16, :] = final[k, :, 0:DL]
        gkr_out[0, k * rows_16:(k + 1) * rows_16, :] = final[k, :, DL:DL + DR]

    dp_copy.wait_recv()
    summed = gwdf[dp] + gwdr[...]
    gwk_out[...] = summed[:, :2 * DN]
    gwv_out[...] = summed[:, 2 * DN:]

    for copy in (
        q_copies + lat_copies + delta_copies + stat_copies + gq_copies + gwx_copies + y_copies
        + gwz_copies + fin_copies + [dp_copy]
    ):
        copy.wait_send()

    def drain(r, carry):
        sib_copy(r).wait_send()

        @pl.when(r > 0)
        def _():
            forward_copy(z_at(r)).wait_send()
            glz_copy(r).wait_send()

        return carry

    lax.fori_loop(0, nz, drain, 0)


def solution(mesh):
    nz = mesh.shape["ctx"] // NX
    nyh = mesh.shape["head"] // CORES

    def shards(*args):
        tok = args[0].shape[1]
        half = tok // CORES
        queries, keys = NX * tok, nz * tok
        sub = DL // (nz * NX)
        rows_y = half // nyh
        wide = DL + 2 * DR
        q_wide = 2 * DN + 2 * DR + 2 * DV
        cols = 2 * DN + 2 * DV
        any_spec = pl.BlockSpec(memory_space=pl.ANY)
        vmem = pl.BlockSpec(memory_space=pltpu.VMEM)
        dma = pltpu.SemaphoreType.DMA
        heads = nyh * CORES
        scratch = [
            pltpu.VMEM((nz, tok, wide), BF16),
            pltpu.VMEM((tok, DR), BF16),
            pltpu.VMEM((NX, tok, q_wide), BF16),
            pltpu.VMEM((tok, 2 * DV), BF16),
            pltpu.VMEM((DL, cols), BF16),
            pltpu.VMEM((NX, 8, tok), F32),
            pltpu.VMEM((8, queries), jnp.int32),
            pltpu.VMEM((2, queries, DN + 2 * DR), BF16),
            pltpu.VMEM((2, queries, DV), BF16),
            pltpu.VMEM((DL, keys), BF16),
            pltpu.VMEM((2, DN + 2 * DR, keys), BF16),
            pltpu.VMEM((2, nz, tok, queries), F32),
            pltpu.VMEM((2, nz, tok, queries), F32),
            pltpu.VMEM((2, nz, 1, queries), F32),
            pltpu.VMEM((2, nz, 1, queries), F32),
            pltpu.VMEM((NX, 8, queries), F32),
            pltpu.VMEM((2, keys, queries), BF16),
            pltpu.VMEM((keys, cols), BF16),
            pltpu.VMEM((nz, tok, wide), BF16),
            pltpu.VMEM((nz, half, wide), BF16),
            pltpu.VMEM((nz, half, wide), BF16),
            pltpu.VMEM((nz, half, wide), BF16),
            pltpu.VMEM((nyh, rows_y, wide), F32),
            pltpu.VMEM((nyh, rows_y, wide), BF16),
            pltpu.VMEM((nyh, rows_y, wide), BF16),
            pltpu.VMEM((heads, rows_y, wide), BF16),
            pltpu.VMEM((queries, 2 * DN + 2 * DR), F32),
            pltpu.VMEM((NX, tok, 2 * DN + 2 * DR), BF16),
            pltpu.VMEM((NX, tok, 2 * DN + 2 * DR), BF16),
            pltpu.VMEM((nz, NX, sub, cols), F32),
            pltpu.VMEM((NX, nz, sub, cols), BF16),
            pltpu.VMEM((NX, nz, sub, cols), BF16),
            pltpu.VMEM((nz, sub, cols), F32),
            pltpu.VMEM((nz, sub, cols), BF16),
            pltpu.VMEM((nz, sub, cols), BF16),
            pltpu.VMEM((2, sub // 2, cols), F32),
            pltpu.VMEM((sub // 2, cols), F32),
            dma((8,)),
            dma((nz,)), dma((nz,)), dma((nz,)), dma((nz,)),
            dma((NX,)), dma((NX,)), dma((NX,)), dma((NX,)), dma((NX,)), dma((NX,)),
            dma((nz,)), dma((nz,)), dma((nz,)), dma((nz,)),
            dma((NX,)), dma((NX,)), dma((NX,)), dma((NX,)), dma((nz,)), dma((nz,)),
            dma((nyh,)), dma((nyh,)), dma((heads,)), dma((heads,)), dma((1,)), dma((1,)),
        ]
        return pl.pallas_call(
            functools.partial(kernel, nz, nyh, tok),
            out_shape=(
                jax.ShapeDtypeStruct((1, tok, 2 * DN), BF16),
                jax.ShapeDtypeStruct((1, tok, 2 * DR), BF16),
                jax.ShapeDtypeStruct((1, tok, DL), BF16),
                jax.ShapeDtypeStruct((1, tok, DR), BF16),
                jax.ShapeDtypeStruct((sub // 2, 2 * DN), F32),
                jax.ShapeDtypeStruct((sub // 2, 2 * DV), F32),
            ),
            in_specs=[any_spec] * 8 + [pl.BlockSpec(memory_space=pltpu.SMEM)],
            out_specs=(vmem,) * 6,
            scratch_shapes=scratch,
            compiler_params=pltpu.CompilerParams(
                collective_id=0, has_side_effects=True, vmem_limit_bytes=56 * 1024 * 1024
            ),
        )(*args)

    return jax.shard_map(
        shards,
        mesh=mesh,
        in_specs=(
            P("dp", "ctx", None),
            P("dp", "ctx", None),
            P("dp", "ctx", "head"),
            P("dp", "ctx", "head"),
            P("dp", "ctx", "head"),
            P("dp", "ctx", "head"),
            P(None, "head"),
            P(None, "head"),
            P(),
        ),
        out_specs=(
            P("dp", "ctx", "head"),
            P("dp", "ctx", "head"),
            P("dp", "ctx", None),
            P("dp", "ctx", None),
            P(("ctx", "dp"), "head"),
            P(("ctx", "dp"), "head"),
        ),
        check_vma=False,
    )
```

time: 733 us -> 77.6 us (0.11)
  the two profiles are of different devices: /device:TPU:16 before, /device:TPU:1 now
where the time goes in v1:
time: 77.6 us; the launch traced here: 77.2 us
  Pallas kernels  69.6 us (90%)
  local copies, waits for them, and re-layouts  7.01 us (9%)
    pallas_call x1, Pallas kernels, shards(): pl.pallas_call(functools.partial(kernel, nz, nyh, tok), out_shape=(jax.Sh...  69.6 us
    unnamed x14, local copies, waits for them, and re-layouts  5.53 us

profile of v1, /device:TPU:1, one launch (start us, length us, event | category | flops | bytes accessed | tf_op | source)
XLA Modules:
  0.0 77.2 jit_solution(12291055975066311606)
XLA Ops:
  0.6 1.4 %copy.15.kr_in = bf16[1,128,64]{2,1,0:T(8,128)(2,1)} copy(bf16[1,128,64]{1,2,0:T(8,128)(2,1)} %param.10) | data formatting | bytes 32768 | tf_op args[1]
  2.1 69.6 %shard_map.136 = (bf16[1,128,256]{2,1,0:T(8,128)(2,1)}, bf16[1,128,128]{2,1,0:T(8,128)(2,1)}, bf16[1,128,512]{2,1,0:T(8,128)(2,1)}, bf16[1,128,64]{2,1,0:T(8,128...) custom-call(bf16[1,128,512]{2,1,0:T(8,128)(2,1)} %lat_in.1, bf16[1,128,64]{2,1,0:T(8,128)(2,1)} %copy.15.kr_in, ...), custom_call_target="tpu_custom_call" | custom-call | tf_op jit(solution)/shard_map/pallas_call | solution.py:475
  71.6 0.0 copy-start
  71.6 1.5 %copy.16 = bf16[1,128,64]{1,2,0:T(8,128)(2,1)} copy(bf16[1,128,64]{2,1,0:T(8,128)(2,1)} %get-tuple-element.9) | data formatting | bytes 32768 | tf_op jit(solution)/shard_map/pallas_call | solution.py:475
  73.1 0.0 copy-start.1
  73.1 1.5 %copy.22 = bf16[1,128,256]{2,1,0:T(8,128)(2,1)} copy(bf16[1,128,256]{2,1,0:T(8,128)(2,1)} %get-tuple-element.18) | data formatting | bytes 131072
  74.6 0.0 copy-done.1
  74.6 0.6 copy.23
  75.2 0.0 copy-done
  75.2 0.0 copy-start.3
  75.2 0.7 copy.24
  75.9 0.0 copy-done.3
  75.9 0.0 copy-start.2
  75.9 0.6 copy.25
  76.5 0.1 copy-done.2
  76.6 0.6 copy.26
Async XLA Ops:
  71.6 3.6 %copy-start = (bf16[1,128,512]{2,1,0:T(8,128)(2,1)S(1)}, bf16[1,128,512]{2,1,0:T(8,128)(2,1)}, u32[]{:S(2)}) copy-start(bf16[1,128,512]{2,1,0:T(8,128)(2,1)} %get-tuple-element.20) | copy-start | bytes 393220
  73.1 1.5 %copy-start.1 = (bf16[1,128,128]{2,1,0:T(8,128)(2,1)S(1)}, bf16[1,128,128]{2,1,0:T(8,128)(2,1)}, u32[]{:S(2)}) copy-start(bf16[1,128,128]{2,1,0:T(8,128)(2,1)} %get-tuple-element.19) | copy-start | bytes 98308
  75.2 0.7 copy-start.3
  75.9 0.7 copy-start.2

commit v2 on v1

--- a/solution.py
+++ b/solution.py
@@ -46,7 +46,8 @@
     pexp, dsx, mscr, lscr, stats, dsall, gall,
     glsend, glsib, glz, glzr, tot, ychunk, yrecv, final,
     gqf, gqb, gqr, gwf, gwb, gwr, gwzf, gwzb, gwzr, gwdf, gwdr,
-    local_sem, lat_s, lat_r, fwd_s, fwd_r, q_s, q_r, de_s, de_r, st_s, st_r,
+    gqn_v, gqr_v, gl_v, gkr_v, gwk_v, gwv_v,
+    local_sem, out_sem, lat_s, lat_r, fwd_s, fwd_r, q_s, q_r, de_s, de_r, st_s, st_r,
     sib_s, sib_r, glz_s, glz_r, gq_s, gq_r, gwx_s, gwx_r, gwz_s, gwz_r,
     y_s, y_r, fin_s, fin_r, dp_s, dp_r,
 ):
@@ -112,7 +113,7 @@
         pl.semaphore_signal(barrier, inc=1, device_id=target, device_id_type=MESH)
     for copy in local:
         copy.wait()
-    rope_lanes = jnp.concatenate([krs[...], jnp.zeros((tok, DR), BF16)], axis=1)
+    rope_lanes = jnp.concatenate([krs[...].T, jnp.zeros((tok, DR), BF16)], axis=1)
     lat[z, :, DL:] = rope_lanes
     pl.semaphore_wait(barrier, len(targets))
 
@@ -334,8 +335,18 @@
     for p in x_peers:
         remote(gqb.at[0], gqr.at[p], gq_s.at[0], gq_r.at[p], at_x(p)).wait_recv()
         mine += gqr[p].astype(F32)
-    gqn_out[0] = mine[:, :2 * DN].astype(BF16)
-    gqr_out[0] = mine[:, 2 * DN:].astype(BF16)
+    gqn_v[...] = mine[:, :2 * DN].astype(BF16)
+    gqr_v[...] = mine[:, 2 * DN:].astype(BF16)
+    out_copies = [
+        pltpu.make_async_copy(gqn_v, gqn_out.at[0], out_sem.at[0]),
+        pltpu.make_async_copy(gqr_v, gqr_out.at[0], out_sem.at[1]),
+        pltpu.make_async_copy(gl_v, gl_out.at[0], out_sem.at[2]),
+        pltpu.make_async_copy(gkr_v, gkr_out.at[0], out_sem.at[3]),
+        pltpu.make_async_copy(gwk_v, gwk_out, out_sem.at[4]),
+        pltpu.make_async_copy(gwv_v, gwv_out, out_sem.at[5]),
+    ]
+    for copy in out_copies[:2]:
+        copy.start()
 
     part = gwf[:, x]
     for p in x_peers:
@@ -383,13 +394,17 @@
         ).wait_recv()
     rows_16 = half // nyh
     for k in range(heads):
-        gl_out[0, k * rows_16:(k + 1) * rows_16, :] = final[k, :, 0:DL]
-        gkr_out[0, k * rows_16:(k + 1) * rows_16, :] = final[k, :, DL:DL + DR]
+        gl_v[k * rows_16:(k + 1) * rows_16, :] = final[k, :, 0:DL]
+    gkr_v[...] = jnp.concatenate([final[k, :, DL:] for k in range(heads)], axis=0).T[:DR]
+    for copy in out_copies[2:4]:
+        copy.start()
 
     dp_copy.wait_recv()
     summed = gwdf[dp] + gwdr[...]
-    gwk_out[...] = summed[:, :2 * DN]
-    gwv_out[...] = summed[:, 2 * DN:]
+    gwk_v[...] = summed[:, :2 * DN]
+    gwv_v[...] = summed[:, 2 * DN:]
+    for copy in out_copies[4:]:
+        copy.start()
 
     for copy in (
         q_copies + lat_copies + delta_copies + stat_copies + gq_copies + gwx_copies + y_copies
@@ -408,6 +423,14 @@
         return carry
 
     lax.fori_loop(0, nz, drain, 0)
+    for copy in out_copies:
+        copy.wait()
+
+
+def hand_over(*refs):
+    count = len(refs) // 2
+    for k in range(count):
+        refs[count + k][...] = refs[k][...]
 
 
 def solution(mesh):
@@ -429,7 +452,7 @@
         heads = nyh * CORES
         scratch = [
             pltpu.VMEM((nz, tok, wide), BF16),
-            pltpu.VMEM((tok, DR), BF16),
+            pltpu.VMEM((DR, tok), BF16),
             pltpu.VMEM((NX, tok, q_wide), BF16),
             pltpu.VMEM((tok, 2 * DV), BF16),
             pltpu.VMEM((DL, cols), BF16),
@@ -465,30 +488,44 @@
             pltpu.VMEM((nz, sub, cols), BF16),
             pltpu.VMEM((2, sub // 2, cols), F32),
             pltpu.VMEM((sub // 2, cols), F32),
-            dma((8,)),
+            pltpu.VMEM((tok, 2 * DN), BF16),
+            pltpu.VMEM((tok, 2 * DR), BF16),
+            pltpu.VMEM((tok, DL), BF16),
+            pltpu.VMEM((DR, tok), BF16),
+            pltpu.VMEM((sub // 2, 2 * DN), F32),
+            pltpu.VMEM((sub // 2, 2 * DV), F32),
+            dma((8,)), dma((6,)),
             dma((nz,)), dma((nz,)), dma((nz,)), dma((nz,)),
             dma((NX,)), dma((NX,)), dma((NX,)), dma((NX,)), dma((NX,)), dma((NX,)),
             dma((nz,)), dma((nz,)), dma((nz,)), dma((nz,)),
             dma((NX,)), dma((NX,)), dma((NX,)), dma((NX,)), dma((nz,)), dma((nz,)),
             dma((nyh,)), dma((nyh,)), dma((heads,)), dma((heads,)), dma((1,)), dma((1,)),
         ]
-        return pl.pallas_call(
+        out_shape = (
+            jax.ShapeDtypeStruct((1, tok, 2 * DN), BF16),
+            jax.ShapeDtypeStruct((1, tok, 2 * DR), BF16),
+            jax.ShapeDtypeStruct((1, tok, DL), BF16),
+            jax.ShapeDtypeStruct((1, DR, tok), BF16),
+            jax.ShapeDtypeStruct((sub // 2, 2 * DN), F32),
+            jax.ShapeDtypeStruct((sub // 2, 2 * DV), F32),
+        )
+        results = pl.pallas_call(
             functools.partial(kernel, nz, nyh, tok),
-            out_shape=(
-                jax.ShapeDtypeStruct((1, tok, 2 * DN), BF16),
-                jax.ShapeDtypeStruct((1, tok, 2 * DR), BF16),
-                jax.ShapeDtypeStruct((1, tok, DL), BF16),
-                jax.ShapeDtypeStruct((1, tok, DR), BF16),
-                jax.ShapeDtypeStruct((sub // 2, 2 * DN), F32),
-                jax.ShapeDtypeStruct((sub // 2, 2 * DV), F32),
-            ),
+            out_shape=out_shape,
             in_specs=[any_spec] * 8 + [pl.BlockSpec(memory_space=pltpu.SMEM)],
-            out_specs=(vmem,) * 6,
+            out_specs=(any_spec,) * 6,
             scratch_shapes=scratch,
             compiler_params=pltpu.CompilerParams(
                 collective_id=0, has_side_effects=True, vmem_limit_bytes=56 * 1024 * 1024
             ),
-        )(*args)
+        )(args[0], jnp.swapaxes(args[1], 1, 2), *args[2:])
+        results = pl.pallas_call(
+            hand_over,
+            out_shape=out_shape,
+            in_specs=[vmem] * 6,
+            out_specs=(vmem,) * 6,
+        )(*results)
+        return (*results[:3], jnp.swapaxes(results[3], 1, 2), *results[4:])
 
     return jax.shard_map(
         shards,

time: 77.6 us -> 71.8 us (0.925)
  local copies, waits for them, and re-layouts: 7.01 us -> 0 us
  Pallas kernels: 69.6 us -> 71 us
    unnamed x14 -> x0, local copies, waits for them, and re-layouts: 5.53 us -> none
    pallas_call x1 -> x0, local copies, waits for them, and re-layouts: 1.48 us -> none  [shards(): pl.pallas_call(functools.partial(kernel, nz, nyh, tok), out_shape=(jax.Sh...]
    pallas_call x1 -> x2, Pallas kernels: 69.6 us -> 71 us  [the longest x1 69.3 us: shards(): pl.pallas_call(functools.partial(kernel, nz, nyh, tok), out_shape=out_sha...]
where the time goes in v2:
time: 71.8 us; the launch traced here: 71.7 us
  Pallas kernels  71 us (99%)
    pallas_call x1, Pallas kernels, shards(): pl.pallas_call(functools.partial(kernel, nz, nyh, tok), out_shape=out_sha...  69.3 us
    pallas_call x1, Pallas kernels, shards(): pl.pallas_call(hand_over, out_shape=out_shape, in_specs=[vmem] * 6, out_s...  1.68 us

profile of v2, /device:TPU:1, one launch (start us, length us, event | category | flops | bytes accessed | tf_op | source)
XLA Modules:
  0.0 71.7 jit_solution(16417001475056288274)
XLA Ops:
  0.6 69.3 %shard_map.136 = (bf16[1,128,256]{2,1,0:T(8,128)(2,1)}, bf16[1,128,128]{2,1,0:T(8,128)(2,1)}, bf16[1,128,512]{2,1,0:T(8,128)(2,1)}, bf16[1,64,128]{2,1,0:T(8,128...) custom-call(bf16[1,128,512]{2,1,0:T(8,128)(2,1)} %lat_in.1, bf16[1,64,128]{2,1,0:T(8,128)(2,1)} %bitcast.2, ...), custom_call_target="tpu_custom_call" | custom-call | tf_op jit(solution)/shard_map/pallas_call | solution.py:512
  70.0 1.7 %shard_map.137 = (bf16[1,128,256]{2,1,0:T(8,128)(2,1)}, bf16[1,128,128]{2,1,0:T(8,128)(2,1)}, bf16[1,128,512]{2,1,0:T(8,128)(2,1)}, bf16[1,64,128]{2,1,0:T(8,128...) custom-call(bf16[1,128,256]{2,1,0:T(8,128)(2,1)} %get-tuple-element.18.refs_0_, ...), custom_call_target="tpu_custom_call" | custom-call | tf_op jit(solution)/shard_map/pallas_call | solution.py:522

commit v3 on v2

v3 whole, which is shorter than its diff:
```python
import functools
import math

import jax
import jax.numpy as jnp
from jax import lax
from jax.experimental import pallas as pl
from jax.experimental.pallas import tpu as pltpu
from jax.sharding import PartitionSpec as P

DL = 512
DN = 128
DR = 64
DV = 128
NX = 4
CORES = 2
HALF_GROUP = 64
LAT_SUBS = 4
SUBS = 2

QW = 2 * DN + 2 * DR + 2 * DV
KW = DN + 2 * DR
CW = 2 * DN + 2 * DV
LW = DL + 2 * DR
GW = 2 * DN + 2 * DR

MESH = pl.DeviceIdType.MESH
MASKED = -1.5e38
FLOOR = -1.0e38
F32 = jnp.float32
BF16 = jnp.bfloat16

NT = (((1,), (1,)), ((), ()))


def dot(a, b):
    return jnp.dot(a, b, preferred_element_type=F32)


def dot_nt(a, b):
    return lax.dot_general(a, b, NT, preferred_element_type=F32)


def kernel(
    nz, nyh, tok,
    lat_in, kr_in, qn_in, qr_in, go_in, so_in, wk_in, wv_in, order,
    gqn_out, gqr_out, gl_out, gkr_out, gwk_out, gwv_out,
    lat, krs, q, saved, w, qpos, qcat, qgo, latt, kcat, vals, keyst,
    pexp, dprob, mscr, lscr, stats, dsall, gall,
    glb, rsend, rrecv, tot, hsend, hsib, ybuf, final,
    gqf, gqsend, gqsib, gqb, gqr, gwf, gwsend, gwsib, gwb, gwr, gwzf, gwzb, gwzr, gwdf, gwdr,
    gqn_v, gqr_v, gl_v, gkr_v, gwk_v, gwv_v,
    local_sem, out_sem, lat_s, lat_r, q_s, q_r, w_s, w_r, st_s, st_r,
    rs_s, rs_r, gqs_s, gqs_r, gws_s, gws_r, gq_s, gq_r, gwx_s, gwx_r, gwz_s, gwz_r,
    half_s, half_r, y_s, y_r, fin_s, fin_r, dp_s, dp_r,
):
    ctx = lax.axis_index("ctx")
    head = lax.axis_index("head")
    dp = lax.axis_index("dp")
    z, x = lax.div(ctx, NX), lax.rem(ctx, NX)
    y, core = lax.div(head, CORES), lax.rem(head, CORES)
    queries = NX * tok
    blocks = nz // 2
    piece = tok // SUBS
    lat_piece = tok // LAT_SUBS
    half = tok // CORES
    score_scale = (DN + DR) ** -0.5
    log2_scale = score_scale * math.log2(math.e)
    sib_head = y * CORES + (1 - core)
    sib = 1 - core

    def at_z(peer):
        return {"ctx": peer * NX + x, "head": head, "dp": dp}

    def at_x(peer, head_index):
        return {"ctx": z * NX + peer, "head": head_index, "dp": dp}

    def at_head(peer):
        return {"ctx": ctx, "head": peer, "dp": dp}

    sibling = at_head(sib_head)
    other_dp = {"ctx": ctx, "head": head, "dp": 1 - dp}

    def remote(src, dst, send, recv, device):
        return pltpu.make_async_remote_copy(
            src_ref=src, dst_ref=dst, send_sem=send, recv_sem=recv,
            device_id=device, device_id_type=MESH,
        )

    def near(i, n):
        return [lax.rem(i + 1, n), lax.rem(i + n - 1, n)] if n > 2 else [1 - i]

    def others(i, n):
        return near(i, n) + [lax.rem(i + k, n) for k in range(2, n - 1)]

    z_peers, x_peers = others(z, nz), others(x, NX)
    x_near, y_near = near(x, NX), near(y, nyh)
    gather_to = at_z(lax.rem(z + (1 - core) * (nz - 1) + core, nz))
    sums_to = at_z(lax.rem(z + (1 - core) + core * (nz - 1), nz))
    y_devices = [at_head(p * CORES + core) for p in y_near]

    local = [
        pltpu.make_async_copy(lat_in.at[0], lat.at[0, :, pl.ds(0, DL)], local_sem.at[0]),
        pltpu.make_async_copy(kr_in.at[0], krs, local_sem.at[1]),
        pltpu.make_async_copy(qn_in.at[0], q.at[core, x, :, pl.ds(0, 2 * DN)], local_sem.at[2]),
        pltpu.make_async_copy(
            qr_in.at[0], q.at[core, x, :, pl.ds(2 * DN, 2 * DR)], local_sem.at[3]
        ),
        pltpu.make_async_copy(
            go_in.at[0], q.at[core, x, :, pl.ds(GW, 2 * DV)], local_sem.at[4]
        ),
        pltpu.make_async_copy(wk_in, w.at[core, :, pl.ds(0, 2 * DN)], local_sem.at[5]),
        pltpu.make_async_copy(wv_in, w.at[core, :, pl.ds(2 * DN, 2 * DV)], local_sem.at[6]),
        pltpu.make_async_copy(so_in.at[0], saved, local_sem.at[7]),
    ]
    for copy in local:
        copy.start()

    barrier = pltpu.get_barrier_semaphore()
    targets = (
        [at_z(p) for p in near(z, nz)] + [at_x(p, head) for p in x_near]
        + [sibling, other_dp] + y_devices
    )
    for target in targets:
        pl.semaphore_signal(barrier, inc=1, device_id=target, device_id_type=MESH)
    for copy in local:
        copy.wait()
    lat[0, :, DL:] = jnp.concatenate([krs[...].T, jnp.zeros((tok, DR), BF16)], axis=1)
    pl.semaphore_wait(barrier, len(targets))

    def lat_copy(m, j):
        rows = pl.ds(j * lat_piece, lat_piece)
        return remote(
            lat.at[m, rows], lat.at[m + 1, rows], lat_s.at[m * LAT_SUBS + j],
            lat_r.at[(m + 1) * LAT_SUBS + j], gather_to,
        )

    def q_copy(p, j, send, device, c=core):
        rows = pl.ds(j * half, half)
        return remote(
            q.at[c, p, rows], q.at[c, p, rows], q_s.at[send], q_r.at[(c * NX + p) * 2 + j], device
        )

    sent = []

    def start(copy):
        copy.start()
        sent.append(copy)

    for j in range(LAT_SUBS):
        start(lat_copy(0, j))
    for j in range(2):
        for k, p in enumerate(x_near):
            start(q_copy(x, (j + k) % 2, 2 * k + j, at_x(p, head)))
    start(remote(w.at[core], w.at[core], w_s.at[0], w_r.at[0], sibling))
    for j in range(2):
        start(q_copy(x, j, 4 + j, sibling))

    product = (q[core, x, :, GW:].astype(F32) * saved[...].astype(F32)).T
    stats[core, x, 0:1, queries // 2:] = jnp.sum(product[:DV], axis=0, keepdims=True)
    stats[core, x, 1:2, queries // 2:] = jnp.sum(product[DV:], axis=0, keepdims=True)

    lane = lax.broadcasted_iota(jnp.int32, (1, tok), 1)
    for p in range(NX):
        first = 2 * (z * NX + p)
        qpos[0:1, p * tok:(p + 1) * tok] = jnp.where(
            lane < HALF_GROUP,
            order[first] * HALF_GROUP + lane,
            order[first + 1] * HALF_GROUP + lane - HALF_GROUP,
        )

    def pass_on(m):
        def take():
            for j in range(LAT_SUBS):
                lat_copy(m - 1, j).wait_recv()
                if m < blocks - 1:
                    start(lat_copy(m, j))
                elif m == blocks - 1:
                    @pl.when(core == 1)
                    def _():
                        lat_copy(m, j).start()

        if m < blocks:
            take()
        else:
            pl.when(core == 1)(take)

    def project(s):
        slot = s + core
        latents = lat[slot, :, 0:DL]
        rope = lat[slot, :, DL:]
        ropes = (rope, jnp.concatenate([rope[:, DR:], rope[:, :DR]], axis=1))
        columns = slice(s * tok, (s + 1) * tok)
        latt[:, columns] = latents.T
        for c in range(CORES):
            projected = dot(latents, w[c]).astype(BF16)
            for h in range(2):
                hh = 2 * c + h
                key = jnp.concatenate([projected[:, h * DN:(h + 1) * DN], ropes[h]], axis=1)
                kcat[hh, columns, :] = key
                keyst[hh, :, columns] = key.T
                vals[hh, columns, :] = projected[:, 2 * DN + h * DV:2 * DN + (h + 1) * DV]

    def q_take(p, j, number, onward=None):
        q_copy(p, j, 0, sibling).wait_recv()
        if onward is not None:
            start(q_copy(p, j, 6 + j, at_x(onward, head)))
        start(q_copy(p, j, 8 + number, sibling))

    def q_first():
        if len(x_near) == 2:
            right, left = x_near
            q_take(left, 0, 0, right)
            q_take(right, 1, 1, left)

    def q_second():
        if len(x_near) == 2:
            right, left = x_near
            q_take(left, 1, 2)
            q_take(right, 0, 3)
        else:
            for j in range(2):
                q_take(x_near[0], j, j)

    def q_third():
        for p in x_peers[2:]:
            for j in range(2):
                q_take(p, j, 4 + j)

    pass_on(1)
    remote(w.at[sib], w.at[sib], w_s.at[0], w_r.at[0], sibling).wait_recv()
    q_first()
    project(0)
    for s in range(1, max(blocks, 4)):
        if s == 3:
            q_third()
        if s < blocks:
            pass_on(s + 1)
        if s == 1:
            q_second()
        if s < blocks:
            project(s)
    for p in range(NX):
        for j in range(2):
            q_copy(p, j, 0, sibling, sib).wait_recv()
    for p in range(NX):
        rows = slice(p * tok, (p + 1) * tok)
        for c in range(CORES):
            for h in range(2):
                qcat[2 * c + h, rows, 0:DN] = q[c, p, :, h * DN:(h + 1) * DN]
                qcat[2 * c + h, rows, DN:] = q[c, p, :, 2 * DN:GW]
                qgo[2 * c + h, rows, :] = q[c, p, :, GW + h * DV:GW + (h + 1) * DV]

    def first_pass(s, carry):
        slot = s + core
        block = lax.rem(z + (1 - core) * slot + core * (nz - slot), nz)
        first = 2 * (block * NX + x)
        rows = pl.ds(pl.multiple_of(s * tok, tok), tok)
        row = lax.broadcasted_iota(jnp.int32, (HALF_GROUP, queries), 0)
        where_q = qpos[0:1, :]
        seen = jnp.concatenate(
            [row <= where_q - order[first + g] * HALF_GROUP for g in range(2)], axis=0
        )
        for hh in range(2 * CORES):
            scores = jnp.where(seen, dot_nt(kcat[hh, rows, :], qcat[hh]) * log2_scale, MASKED)
            top = jnp.maximum(jnp.max(scores, axis=0, keepdims=True), FLOOR)
            weight = jnp.exp2(scores - top)
            mscr[hh, s] = top
            lscr[hh, s] = jnp.sum(weight, axis=0, keepdims=True)
            pexp[hh, s] = weight
            dprob[hh, s] = dot_nt(vals[hh, rows, :], qgo[hh])
        return carry

    lax.fori_loop(0, blocks, first_pass, 0)

    for hh in range(2 * CORES):
        top = mscr[hh, 0]
        for s in range(1, blocks):
            top = jnp.maximum(top, mscr[hh, s])
        total = jnp.zeros_like(top)
        for s in range(blocks):
            total += lscr[hh, s] * jnp.exp2(mscr[hh, s] - top)
        summary = top + jnp.log2(jnp.maximum(total, 1e-37))
        stats[core, x, 2 * hh:2 * hh + 1, 0:queries // 2] = summary[:, :queries // 2]
        stats[core, x, 2 * hh + 1:2 * hh + 2, 0:queries // 2] = summary[:, queries // 2:]
    partners = [(core, p, at_x(p, head)) for p in x_peers]
    partners += [(sib, p, at_x(p, sib_head)) for p in x_peers] + [(sib, x, sibling)]
    mine = core * NX + x
    for k, (_, _, device) in enumerate(partners):
        start(remote(stats.at[core, x], stats.at[core, x], st_s.at[k], st_r.at[mine], device))
    for c, p, device in partners:
        remote(
            stats.at[c, p], stats.at[c, p], st_s.at[0], st_r.at[c * NX + p], device
        ).wait_recv()
    log_total, row_delta = [], []
    everyone = [(c, p) for c in range(CORES) for p in range(NX)]
    for hh in range(2 * CORES):
        sums = [
            jnp.concatenate(
                [stats[c, p, 2 * hh + k:2 * hh + k + 1, 0:queries // 2] for k in range(2)], axis=1
            )
            for c, p in everyone
        ]
        top = functools.reduce(jnp.maximum, sums)
        total = functools.reduce(jnp.add, [jnp.exp2(one - top) for one in sums])
        log_total.append(top + jnp.log2(total))
        row_delta.append(jnp.concatenate(
            [stats[hh // 2, p, hh % 2:hh % 2 + 1, queries // 2:] for p in range(NX)], axis=1
        ))

    def block_sums(t):
        s = blocks - 1 - t
        rows = slice(s * tok, (s + 1) * tok)
        ropes = []
        latent_sum = None
        for c in range(CORES):
            key_parts, value_parts = [], []
            for hh in (2 * c, 2 * c + 1):
                factor = jnp.exp2(mscr[hh, s] - log_total[hh])
                probs = pexp[hh, s] * factor
                dscores = (probs * ((dprob[hh, s] - row_delta[hh]) * score_scale)).astype(BF16)
                dsall[hh, rows, :] = dscores
                joint = dot(dscores, qcat[hh])
                key_parts.append(joint[:, :DN].astype(BF16))
                ropes.append(joint[:, DN:])
                value_parts.append(dot(probs.astype(BF16), qgo[hh]).astype(BF16))
            grads = jnp.concatenate(key_parts + value_parts, axis=1)
            gall[c, rows, :] = grads
            part = dot_nt(grads, w[c])
            latent_sum = part if latent_sum is None else latent_sum + part
        glb[t, :, 0:DL] = latent_sum
        glb[t, :, DL:] = jnp.where(
            lax.broadcasted_iota(jnp.int32, (tok, 2 * DR), 1) < DR,
            ropes[0] + ropes[2], ropes[1] + ropes[3],
        )

    def ring_copy(t, j):
        rows = pl.ds(j * piece, piece)
        return remote(
            rsend.at[t, rows], rrecv.at[t, rows], rs_s.at[t * SUBS + j], rs_r.at[t * SUBS + j],
            sums_to,
        )

    def ring_step(t):
        for j in range(SUBS):
            rows = slice(j * piece, (j + 1) * piece)
            so_far = glb[t, rows, :]
            if t > 0:
                ring_copy(t - 1, j).wait_recv()
                so_far = so_far + rrecv[t - 1, rows, :].astype(F32)
            rsend[t, rows, :] = so_far.astype(BF16)
            if t < blocks - 1:
                start(ring_copy(t, j))
            else:
                tot[rows, :] = so_far

                @pl.when(core == 1)
                def _():
                    ring_copy(t, j).start()

        if t == blocks - 1:
            @pl.when(core == 0)
            def _():
                hsend[...] = tot[half:, :].astype(BF16)
                half_copy(hsend).start()

    def half_copy(source):
        return remote(source, hsib, half_s.at[0], half_r.at[0], sibling)

    def query_grads(c):
        parts = [dot(keyst[2 * c + h], dsall[2 * c + h]) for h in range(2)]
        return jnp.concatenate(
            [parts[0][:DN], parts[1][:DN], parts[0][DN:] + parts[1][DN:]], axis=0
        ).T

    gq_pass = remote(gqsend, gqsib, gqs_s.at[0], gqs_r.at[0], sibling)
    gw_pass = remote(gwsend, gwsib, gws_s.at[0], gws_r.at[0], sibling)

    def sibling_query_grads():
        gqsend[...] = query_grads(sib).astype(BF16).reshape(gqsend.shape)
        start(gq_pass)

    def sibling_weight_grads():
        gwsend[...] = dot(latt[...], gall[sib]).astype(BF16).reshape(gwsend.shape)
        start(gw_pass)

    def own_weight_grads():
        gwf[...] = dot(latt[...], gall[core]).reshape(gwf.shape)
        gw_pass.wait_recv()
        gwf[...] += gwsib[...].astype(F32)
        for p in range(NX):
            gwb[p] = gwf[:, p].astype(BF16)
        for k, p in enumerate(x_peers):
            start(remote(gwb.at[p], gwr.at[x], gwx_s.at[k], gwx_r.at[x], at_x(p, head)))

    def own_query_grads():
        own_queries = query_grads(core).reshape(gqf.shape)
        gq_pass.wait_recv()
        gqf[...] = own_queries + gqsib[...].astype(F32)
        gqb[...] = gqf[...].astype(BF16)
        for k, p in enumerate(x_peers):
            start(remote(gqb.at[p], gqr.at[x], gq_s.at[k], gq_r.at[x], at_x(p, head)))

    between = [[functools.partial(block_sums, t) for t in range(1, min(blocks, 3))]]
    between += [[functools.partial(block_sums, t)] for t in range(3, blocks)]
    while len(between) < 3:
        between.append([])
    between[1] += [sibling_weight_grads]
    between[2] += [sibling_query_grads, own_weight_grads]
    block_sums(0)
    ring_step(0)
    for t in range(1, blocks):
        for item in between.pop(0):
            item()
        ring_step(t)
    for item in sum(between, []):
        item()
    own_query_grads()

    own_rows = pl.ds(pl.multiple_of(core * half, half), half)

    @pl.when(core == 1)
    def _():
        for j in range(SUBS):
            ring_copy(blocks - 1, j).wait_recv()
            if j == SUBS // 2 - 1:
                half_copy(rrecv.at[blocks - 1, pl.ds(0, half)]).start()
        tot[half:, :] = rrecv[blocks - 1, half:, :].astype(F32)

    half_copy(hsend).wait_recv()
    ybuf[y] = (tot[own_rows, :] + hsib[...].astype(F32)).astype(BF16)

    yhalf = half // 2

    def y_copy(slot, j, send, device):
        rows = pl.ds(j * yhalf, yhalf)
        return remote(
            ybuf.at[slot, rows], ybuf.at[slot, rows], y_s.at[send], y_r.at[2 * slot + j], device
        )

    for j in range(2):
        for k, device in enumerate(y_devices):
            start(y_copy(y, (j + k) % 2, 2 * k + j, device))

    part = gwf[:, x]
    for p in x_peers:
        remote(gwb.at[0], gwr.at[p], gwx_s.at[0], gwx_r.at[p], at_x(p, head)).wait_recv()
        part += gwr[p].astype(F32)
    gwzf[...] = part
    gwzb[...] = part.astype(BF16)
    for k, p in enumerate(z_peers):
        start(remote(gwzb.at[p], gwzr.at[z], gwz_s.at[k], gwz_r.at[z], at_z(p)))

    if nyh > 2:
        right, left = y_near
        y_copy(left, 0, 0, sibling).wait_recv()
        start(y_copy(left, 0, 4, y_devices[0]))
        y_copy(right, 1, 0, sibling).wait_recv()
        start(y_copy(right, 1, 5, y_devices[1]))

    part = gqf[x]
    for p in x_peers:
        remote(gqb.at[0], gqr.at[p], gq_s.at[0], gq_r.at[p], at_x(p, head)).wait_recv()
        part += gqr[p].astype(F32)
    gqn_v[...] = part[:, :2 * DN].astype(BF16)
    gqr_v[...] = part[:, 2 * DN:].astype(BF16)
    out_copies = [
        pltpu.make_async_copy(gqn_v, gqn_out.at[0], out_sem.at[0]),
        pltpu.make_async_copy(gqr_v, gqr_out.at[0], out_sem.at[1]),
        pltpu.make_async_copy(gl_v, gl_out.at[0], out_sem.at[2]),
        pltpu.make_async_copy(gkr_v, gkr_out.at[0], out_sem.at[3]),
        pltpu.make_async_copy(gwk_v, gwk_out, out_sem.at[4]),
        pltpu.make_async_copy(gwv_v, gwv_out, out_sem.at[5]),
    ]
    for copy in out_copies[:2]:
        copy.start()

    part = gwzf[z]
    for p in z_peers:
        remote(gwzb.at[0], gwzr.at[p], gwz_s.at[0], gwz_r.at[p], at_z(p)).wait_recv()
        part += gwzr[p].astype(F32)
    gwdf[...] = part.reshape(gwdf.shape)
    dp_copy = remote(gwdf.at[1 - dp], gwdr, dp_s.at[0], dp_r.at[0], other_dp)
    start(dp_copy)

    if nyh > 2:
        y_copy(left, 1, 0, sibling).wait_recv()
        y_copy(right, 0, 0, sibling).wait_recv()
        far = others(y, nyh)[2]
        for j in range(2):
            y_copy(far, j, 0, sibling).wait_recv()
    else:
        for j in range(2):
            y_copy(y_near[0], j, 0, sibling).wait_recv()
    part = functools.reduce(jnp.add, [ybuf[k].astype(F32) for k in range(nyh)])
    folded = part[:, DL:] + jnp.concatenate([part[:, DL + DR:], part[:, DL:DL + DR]], axis=1)
    final[core, :, 0:DL] = part[:, :DL].astype(BF16)
    final[core, :, DL:] = folded.astype(BF16)
    start(remote(final.at[core], final.at[core], fin_s.at[0], fin_r.at[core], sibling))

    dp_copy.wait_recv()
    summed = gwdf[dp] + gwdr[...]
    gwk_v[...] = summed[:, :2 * DN]
    gwv_v[...] = summed[:, 2 * DN:]
    for copy in out_copies[4:]:
        copy.start()

    remote(final.at[sib], final.at[sib], fin_s.at[0], fin_r.at[sib], sibling).wait_recv()
    gl_v[...] = jnp.concatenate([final[c, :, 0:DL] for c in range(CORES)], axis=0)
    gkr_v[...] = jnp.concatenate([final[c, :, DL:] for c in range(CORES)], axis=0).T[:DR]
    for copy in out_copies[2:4]:
        copy.start()

    for copy in sent:
        copy.wait_send()
    half_copy(hsend).wait_send()

    @pl.when(core == 1)
    def _():
        for j in range(LAT_SUBS):
            lat_copy(blocks - 1, j).wait_send()
        for j in range(SUBS):
            ring_copy(blocks - 1, j).wait_send()

    for copy in out_copies:
        copy.wait()


def hand_over(*refs):
    count = len(refs) // 2
    for k in range(count):
        refs[count + k][...] = refs[k][...]


def solution(mesh):
    nz = mesh.shape["ctx"] // NX
    nyh = mesh.shape["head"] // CORES

    def shards(*args):
        tok = args[0].shape[1]
        queries = NX * tok
        blocks = nz // 2
        keys = blocks * tok
        sub = DL // (nz * NX)
        any_spec = pl.BlockSpec(memory_space=pl.ANY)
        vmem = pl.BlockSpec(memory_space=pltpu.VMEM)
        dma = pltpu.SemaphoreType.DMA
        scratch = [
            pltpu.VMEM((blocks + 1, tok, LW), BF16),
            pltpu.VMEM((DR, tok), BF16),
            pltpu.VMEM((CORES, NX, tok, QW), BF16),
            pltpu.VMEM((tok, 2 * DV), BF16),
            pltpu.VMEM((CORES, DL, CW), BF16),
            pltpu.VMEM((8, queries), jnp.int32),
            pltpu.VMEM((4, queries, KW), BF16),
            pltpu.VMEM((4, queries, DV), BF16),
            pltpu.VMEM((DL, keys), BF16),
            pltpu.VMEM((4, keys, KW), BF16),
            pltpu.VMEM((4, keys, DV), BF16),
            pltpu.VMEM((4, KW, keys), BF16),
            pltpu.VMEM((4, blocks, tok, queries), F32),
            pltpu.VMEM((4, blocks, tok, queries), F32),
            pltpu.VMEM((4, blocks, 1, queries), F32),
            pltpu.VMEM((4, blocks, 1, queries), F32),
            pltpu.VMEM((CORES, NX, 8, queries // 2 + tok), F32),
            pltpu.VMEM((4, keys, queries), BF16),
            pltpu.VMEM((CORES, keys, CW), BF16),
            pltpu.VMEM((blocks, tok, LW), F32),
            pltpu.VMEM((blocks, tok, LW), BF16),
            pltpu.VMEM((blocks, tok, LW), BF16),
            pltpu.VMEM((tok, LW), F32),
            pltpu.VMEM((tok // CORES, LW), BF16),
            pltpu.VMEM((tok // CORES, LW), BF16),
            pltpu.VMEM((nyh, tok // CORES, LW), BF16),
            pltpu.VMEM((CORES, tok // CORES, LW), BF16),
            pltpu.VMEM((NX, tok, GW), F32),
            pltpu.VMEM((NX, tok, GW), BF16),
            pltpu.VMEM((NX, tok, GW), BF16),
            pltpu.VMEM((NX, tok, GW), BF16),
            pltpu.VMEM((NX, tok, GW), BF16),
            pltpu.VMEM((nz, NX, sub, CW), F32),
            pltpu.VMEM((nz, NX, sub, CW), BF16),
            pltpu.VMEM((nz, NX, sub, CW), BF16),
            pltpu.VMEM((NX, nz, sub, CW), BF16),
            pltpu.VMEM((NX, nz, sub, CW), BF16),
            pltpu.VMEM((nz, sub, CW), F32),
            pltpu.VMEM((nz, sub, CW), BF16),
            pltpu.VMEM((nz, sub, CW), BF16),
            pltpu.VMEM((2, sub // 2, CW), F32),
            pltpu.VMEM((sub // 2, CW), F32),
            pltpu.VMEM((tok, 2 * DN), BF16),
            pltpu.VMEM((tok, 2 * DR), BF16),
            pltpu.VMEM((tok, DL), BF16),
            pltpu.VMEM((DR, tok), BF16),
            pltpu.VMEM((sub // 2, 2 * DN), F32),
            pltpu.VMEM((sub // 2, 2 * DV), F32),
            dma((8,)), dma((6,)),
            dma((LAT_SUBS * (blocks + 1),)), dma((LAT_SUBS * (blocks + 1),)),
            dma((14,)), dma((2 * CORES * NX,)), dma((1,)), dma((1,)),
            dma((CORES * NX,)), dma((CORES * NX,)),
            dma((SUBS * blocks,)), dma((SUBS * blocks,)),
            dma((1,)), dma((1,)), dma((1,)), dma((1,)),
            dma((NX,)), dma((NX,)), dma((NX,)), dma((NX,)), dma((nz,)), dma((nz,)),
            dma((1,)), dma((1,)), dma((6,)), dma((2 * nyh,)),
            dma((1,)), dma((CORES,)), dma((1,)), dma((1,)),
        ]
        out_shape = (
            jax.ShapeDtypeStruct((1, tok, 2 * DN), BF16),
            jax.ShapeDtypeStruct((1, tok, 2 * DR), BF16),
            jax.ShapeDtypeStruct((1, tok, DL), BF16),
            jax.ShapeDtypeStruct((1, DR, tok), BF16),
            jax.ShapeDtypeStruct((sub // 2, 2 * DN), F32),
            jax.ShapeDtypeStruct((sub // 2, 2 * DV), F32),
        )
        results = pl.pallas_call(
            functools.partial(kernel, nz, nyh, tok),
            out_shape=out_shape,
            in_specs=[any_spec] * 8 + [pl.BlockSpec(memory_space=pltpu.SMEM)],
            out_specs=(any_spec,) * 6,
            scratch_shapes=scratch,
            compiler_params=pltpu.CompilerParams(
                collective_id=0, has_side_effects=True, vmem_limit_bytes=56 * 1024 * 1024
            ),
        )(args[0], jnp.swapaxes(args[1], 1, 2), *args[2:])
        results = pl.pallas_call(
            hand_over,
            out_shape=out_shape,
            in_specs=[vmem] * 6,
            out_specs=(vmem,) * 6,
        )(*results)
        return (*results[:3], jnp.swapaxes(results[3], 1, 2), *results[4:])

    return jax.shard_map(
        shards,
        mesh=mesh,
        in_specs=(
            P("dp", "ctx", None),
            P("dp", "ctx", None),
            P("dp", "ctx", "head"),
            P("dp", "ctx", "head"),
            P("dp", "ctx", "head"),
            P("dp", "ctx", "head"),
            P(None, "head"),
            P(None, "head"),
            P(),
        ),
        out_specs=(
            P("dp", "ctx", "head"),
            P("dp", "ctx", "head"),
            P("dp", "ctx", None),
            P("dp", "ctx", None),
            P(("ctx", "dp"), "head"),
            P(("ctx", "dp"), "head"),
        ),
        check_vma=False,
    )
```

time: 71.8 us -> 64.4 us (0.90)
  Pallas kernels: 71 us -> 63.6 us
    pallas_call x1, Pallas kernels: 69.3 us -> 61.9 us  [shards(): pl.pallas_call(functools.partial(kernel, nz, nyh, tok), out_shape=out_sha...]
where the time goes in v3:
time: 64.4 us; the launch traced here: 64.2 us
  Pallas kernels  63.6 us (99%)
    pallas_call x1, Pallas kernels, shards(): pl.pallas_call(functools.partial(kernel, nz, nyh, tok), out_shape=out_sha...  61.9 us
    pallas_call x1, Pallas kernels, shards(): pl.pallas_call(hand_over, out_shape=out_shape, in_specs=[vmem] * 6, out_s...  1.68 us

profile of v3, /device:TPU:1, one launch (start us, length us, event | category | flops | bytes accessed | tf_op | source)
XLA Modules:
  0.0 64.2 jit_solution(16437111997165733007)
XLA Ops:
  0.6 61.9 %shard_map.136 = (bf16[1,128,256]{2,1,0:T(8,128)(2,1)}, bf16[1,128,128]{2,1,0:T(8,128)(2,1)}, bf16[1,128,512]{2,1,0:T(8,128)(2,1)}, bf16[1,64,128]{2,1,0:T(8,128...) custom-call(bf16[1,128,512]{2,1,0:T(8,128)(2,1)} %lat_in.1, bf16[1,64,128]{2,1,0:T(8,128)(2,1)} %bitcast.2, ...), custom_call_target="tpu_custom_call" | custom-call | tf_op jit(solution)/shard_map/pallas_call | solution.py:615
  62.5 1.7 %shard_map.137 = (bf16[1,128,256]{2,1,0:T(8,128)(2,1)}, bf16[1,128,128]{2,1,0:T(8,128)(2,1)}, bf16[1,128,512]{2,1,0:T(8,128)(2,1)}, bf16[1,64,128]{2,1,0:T(8,128...) custom-call(bf16[1,128,256]{2,1,0:T(8,128)(2,1)} %get-tuple-element.18.refs_0_, ...), custom_call_target="tpu_custom_call" | custom-call | tf_op jit(solution)/shard_map/pallas_call | solution.py:625

commit v4 on v3

--- a/solution.py
+++ b/solution.py
@@ -16,7 +16,7 @@
 CORES = 2
 HALF_GROUP = 64
 LAT_SUBS = 4
-SUBS = 2
+SUBS = 4
 
 QW = 2 * DN + 2 * DR + 2 * DV
 KW = DN + 2 * DR
@@ -48,7 +48,7 @@
     lat, krs, q, saved, w, qpos, qcat, qgo, latt, kcat, vals, keyst,
     pexp, dprob, mscr, lscr, stats, dsall, gall,
     glb, rsend, rrecv, tot, hsend, hsib, ybuf, final,
-    gqf, gqsend, gqsib, gqb, gqr, gwf, gwsend, gwsib, gwb, gwr, gwzf, gwzb, gwzr, gwdf, gwdr,
+    gqf, gqsend, gqsib, gqb, gqr, gqfar, gwf, gwsend, gwsib, gwb, gwr, gwfar, gwzf, gwzb, gwzr, gwdf, gwdr,
     gqn_v, gqr_v, gl_v, gkr_v, gwk_v, gwv_v,
     local_sem, out_sem, lat_s, lat_r, q_s, q_r, w_s, w_r, st_s, st_r,
     rs_s, rs_r, gqs_s, gqs_r, gws_s, gws_r, gq_s, gq_r, gwx_s, gwx_r, gwz_s, gwz_r,
@@ -113,9 +113,6 @@
         pltpu.make_async_copy(wv_in, w.at[core, :, pl.ds(2 * DN, 2 * DV)], local_sem.at[6]),
         pltpu.make_async_copy(so_in.at[0], saved, local_sem.at[7]),
     ]
-    for copy in local:
-        copy.start()
-
     barrier = pltpu.get_barrier_semaphore()
     targets = (
         [at_z(p) for p in near(z, nz)] + [at_x(p, head) for p in x_near]
@@ -124,8 +121,12 @@
     for target in targets:
         pl.semaphore_signal(barrier, inc=1, device_id=target, device_id_type=MESH)
     for copy in local:
+        copy.start()
+    for copy in local[:2]:
         copy.wait()
     lat[0, :, DL:] = jnp.concatenate([krs[...].T, jnp.zeros((tok, DR), BF16)], axis=1)
+    for copy in local[2:5]:
+        copy.wait()
     pl.semaphore_wait(barrier, len(targets))
 
     def lat_copy(m, j):
@@ -152,6 +153,8 @@
     for j in range(2):
         for k, p in enumerate(x_near):
             start(q_copy(x, (j + k) % 2, 2 * k + j, at_x(p, head)))
+    for copy in local[5:]:
+        copy.wait()
     start(remote(w.at[core], w.at[core], w_s.at[0], w_r.at[0], sibling))
     for j in range(2):
         start(q_copy(x, j, 4 + j, sibling))
@@ -268,7 +271,6 @@
             mscr[hh, s] = top
             lscr[hh, s] = jnp.sum(weight, axis=0, keepdims=True)
             pexp[hh, s] = weight
-            dprob[hh, s] = dot_nt(vals[hh, rows, :], qgo[hh])
         return carry
 
     lax.fori_loop(0, blocks, first_pass, 0)
@@ -288,6 +290,14 @@
     mine = core * NX + x
     for k, (_, _, device) in enumerate(partners):
         start(remote(stats.at[core, x], stats.at[core, x], st_s.at[k], st_r.at[mine], device))
+
+    def cotangents(s, carry):
+        rows = pl.ds(pl.multiple_of(s * tok, tok), tok)
+        for hh in range(2 * CORES):
+            dprob[hh, s] = dot_nt(vals[hh, rows, :], qgo[hh])
+        return carry
+
+    lax.fori_loop(0, blocks, cotangents, 0)
     for c, p, device in partners:
         remote(
             stats.at[c, p], stats.at[c, p], st_s.at[0], st_r.at[c * NX + p], device
@@ -384,22 +394,75 @@
         gwsend[...] = dot(latt[...], gall[sib]).astype(BF16).reshape(gwsend.shape)
         start(gw_pass)
 
+    class Scatter:
+        def __init__(self, blocks, arrived, far, send, recv):
+            self.blocks, self.arrived, self.far = blocks, arrived, far
+            self.send, self.recv = send, recv
+            self.size = far.shape[1]
+
+        def copy(self, src, dst, k, kind):
+            return remote(
+                src, dst, self.send.at[3 * k + kind], self.recv.at[3 * k + kind],
+                at_x(x_near[k], head),
+            )
+
+        def part(self, ref, j):
+            return ref.at[pl.ds(j * self.size, self.size)]
+
+        def far_copy(self, k):
+            return self.copy(
+                self.part(self.blocks.at[lax.rem(x + 2, NX)], k), self.far.at[k], k, 0
+            )
+
+        def near_copy(self, k, kind):
+            j = k if kind == 2 else 1 - k
+            return self.copy(
+                self.part(self.blocks.at[x_near[k]], j), self.part(self.arrived.at[k], j), k, kind
+            )
+
+        def begin(self):
+            if len(x_near) == 2:
+                for k in range(2):
+                    start(self.far_copy(k))
+            for k in range(len(x_near)):
+                start(self.near_copy(k, 1))
+                if len(x_near) == 1:
+                    start(self.near_copy(k, 2))
+
+        def pass_on(self):
+            if len(x_near) == 2:
+                for k in range(2):
+                    self.far_copy(k).wait_recv()
+                    rows = slice(k * self.size, (k + 1) * self.size)
+                    p = x_near[k]
+                    self.blocks[p, rows] = (
+                        self.blocks[p, rows].astype(F32) + self.far[k].astype(F32)
+                    ).astype(BF16)
+                    start(self.near_copy(k, 2))
+
+        def finish(self, own):
+            for k in range(len(x_near)):
+                for kind in (1, 2):
+                    self.near_copy(k, kind).wait_recv()
+                own += self.arrived[k].astype(F32)
+            return own
+
+    gw_scatter = Scatter(gwb, gwr, gwfar, gwx_s, gwx_r)
+    gq_scatter = Scatter(gqb, gqr, gqfar, gq_s, gq_r)
+
     def own_weight_grads():
         gwf[...] = dot(latt[...], gall[core]).reshape(gwf.shape)
         gw_pass.wait_recv()
         gwf[...] += gwsib[...].astype(F32)
         for p in range(NX):
             gwb[p] = gwf[:, p].astype(BF16)
-        for k, p in enumerate(x_peers):
-            start(remote(gwb.at[p], gwr.at[x], gwx_s.at[k], gwx_r.at[x], at_x(p, head)))
+        gw_scatter.begin()
 
     def own_query_grads():
         own_queries = query_grads(core).reshape(gqf.shape)
         gq_pass.wait_recv()
         gqf[...] = own_queries + gqsib[...].astype(F32)
         gqb[...] = gqf[...].astype(BF16)
-        for k, p in enumerate(x_peers):
-            start(remote(gqb.at[p], gqr.at[x], gq_s.at[k], gq_r.at[x], at_x(p, head)))
 
     between = [[functools.partial(block_sums, t) for t in range(1, min(blocks, 3))]]
     between += [[functools.partial(block_sums, t)] for t in range(3, blocks)]
@@ -416,6 +479,8 @@
     for item in sum(between, []):
         item()
     own_query_grads()
+    gw_scatter.pass_on()
+    gq_scatter.begin()
 
     own_rows = pl.ds(pl.multiple_of(core * half, half), half)
 
@@ -442,15 +507,13 @@
         for k, device in enumerate(y_devices):
             start(y_copy(y, (j + k) % 2, 2 * k + j, device))
 
-    part = gwf[:, x]
-    for p in x_peers:
-        remote(gwb.at[0], gwr.at[p], gwx_s.at[0], gwx_r.at[p], at_x(p, head)).wait_recv()
-        part += gwr[p].astype(F32)
+    part = gw_scatter.finish(gwf[:, x])
     gwzf[...] = part
     gwzb[...] = part.astype(BF16)
     for k, p in enumerate(z_peers):
         start(remote(gwzb.at[p], gwzr.at[z], gwz_s.at[k], gwz_r.at[z], at_z(p)))
 
+    gq_scatter.pass_on()
     if nyh > 2:
         right, left = y_near
         y_copy(left, 0, 0, sibling).wait_recv()
@@ -458,10 +521,7 @@
         y_copy(right, 1, 0, sibling).wait_recv()
         start(y_copy(right, 1, 5, y_devices[1]))
 
-    part = gqf[x]
-    for p in x_peers:
-        remote(gqb.at[0], gqr.at[p], gq_s.at[0], gq_r.at[p], at_x(p, head)).wait_recv()
-        part += gqr[p].astype(F32)
+    part = gq_scatter.finish(gqf[x])
     gqn_v[...] = part[:, :2 * DN].astype(BF16)
     gqr_v[...] = part[:, 2 * DN:].astype(BF16)
     out_copies = [
@@ -577,12 +637,14 @@
             pltpu.VMEM((NX, tok, GW), BF16),
             pltpu.VMEM((NX, tok, GW), BF16),
             pltpu.VMEM((NX, tok, GW), BF16),
-            pltpu.VMEM((NX, tok, GW), BF16),
+            pltpu.VMEM((2, tok, GW), BF16),
+            pltpu.VMEM((2, tok // 2, GW), BF16),
             pltpu.VMEM((nz, NX, sub, CW), F32),
             pltpu.VMEM((nz, NX, sub, CW), BF16),
             pltpu.VMEM((nz, NX, sub, CW), BF16),
             pltpu.VMEM((NX, nz, sub, CW), BF16),
-            pltpu.VMEM((NX, nz, sub, CW), BF16),
+            pltpu.VMEM((2, nz, sub, CW), BF16),
+            pltpu.VMEM((2, nz // 2, sub, CW), BF16),
             pltpu.VMEM((nz, sub, CW), F32),
             pltpu.VMEM((nz, sub, CW), BF16),
             pltpu.VMEM((nz, sub, CW), BF16),
@@ -600,7 +662,7 @@
             dma((CORES * NX,)), dma((CORES * NX,)),
             dma((SUBS * blocks,)), dma((SUBS * blocks,)),
             dma((1,)), dma((1,)), dma((1,)), dma((1,)),
-            dma((NX,)), dma((NX,)), dma((NX,)), dma((NX,)), dma((nz,)), dma((nz,)),
+            dma((6,)), dma((6,)), dma((6,)), dma((6,)), dma((nz,)), dma((nz,)),
             dma((1,)), dma((1,)), dma((6,)), dma((2 * nyh,)),
             dma((1,)), dma((CORES,)), dma((1,)), dma((1,)),
         ]

time: 64.4 us -> 62.6 us (0.972)
  Pallas kernels: 63.6 us -> 61.8 us
    pallas_call x1, Pallas kernels: 61.9 us -> 60.1 us  [shards(): pl.pallas_call(functools.partial(kernel, nz, nyh, tok), out_shape=out_sha...]
where the time goes in v4:
time: 62.6 us; the launch traced here: 62.4 us
  Pallas kernels  61.8 us (99%)
  between operations  0.64 us (1%)
    pallas_call x1, Pallas kernels, shards(): pl.pallas_call(functools.partial(kernel, nz, nyh, tok), out_shape=out_sha...  60.1 us
    pallas_call x1, Pallas kernels, shards(): pl.pallas_call(hand_over, out_shape=out_shape, in_specs=[vmem] * 6, out_s...  1.68 us

profile of v4, /device:TPU:1, one launch (start us, length us, event | category | flops | bytes accessed | tf_op | source)
XLA Modules:
  0.0 62.4 jit_solution(1280912916150504292)
XLA Ops:
  0.6 60.1 %shard_map.136 = (bf16[1,128,256]{2,1,0:T(8,128)(2,1)}, bf16[1,128,128]{2,1,0:T(8,128)(2,1)}, bf16[1,128,512]{2,1,0:T(8,128)(2,1)}, bf16[1,64,128]{2,1,0:T(8,128...) custom-call(bf16[1,128,512]{2,1,0:T(8,128)(2,1)} %lat_in.1, bf16[1,64,128]{2,1,0:T(8,128)(2,1)} %bitcast.2, ...), custom_call_target="tpu_custom_call" | custom-call | tf_op jit(solution)/shard_map/pallas_call | solution.py:677
  60.8 1.7 %shard_map.137 = (bf16[1,128,256]{2,1,0:T(8,128)(2,1)}, bf16[1,128,128]{2,1,0:T(8,128)(2,1)}, bf16[1,128,512]{2,1,0:T(8,128)(2,1)}, bf16[1,64,128]{2,1,0:T(8,128...) custom-call(bf16[1,128,256]{2,1,0:T(8,128)(2,1)} %get-tuple-element.18.refs_0_, ...), custom_call_target="tpu_custom_call" | custom-call | tf_op jit(solution)/shard_map/pallas_call | solution.py:687

commit v5 on v4

--- a/solution.py
+++ b/solution.py
@@ -285,8 +285,10 @@
         summary = top + jnp.log2(jnp.maximum(total, 1e-37))
         stats[core, x, 2 * hh:2 * hh + 1, 0:queries // 2] = summary[:, :queries // 2]
         stats[core, x, 2 * hh + 1:2 * hh + 2, 0:queries // 2] = summary[:, queries // 2:]
-    partners = [(core, p, at_x(p, head)) for p in x_peers]
-    partners += [(sib, p, at_x(p, sib_head)) for p in x_peers] + [(sib, x, sibling)]
+    partners = []
+    for p in reversed(x_peers):
+        partners += [(core, p, at_x(p, head)), (sib, p, at_x(p, sib_head))]
+    partners.append((sib, x, sibling))
     mine = core * NX + x
     for k, (_, _, device) in enumerate(partners):
         start(remote(stats.at[core, x], stats.at[core, x], st_s.at[k], st_r.at[mine], device))
@@ -372,10 +374,14 @@
             @pl.when(core == 0)
             def _():
                 hsend[...] = tot[half:, :].astype(BF16)
-                half_copy(hsend).start()
-
-    def half_copy(source):
-        return remote(source, hsib, half_s.at[0], half_r.at[0], sibling)
+                for j in range(2):
+                    half_copy(hsend.at[pl.ds(j * yhalf, yhalf)], j).start()
+
+    yhalf = half // 2
+
+    def half_copy(source, j):
+        rows = pl.ds(j * yhalf, yhalf)
+        return remote(source, hsib.at[rows], half_s.at[j], half_r.at[j], sibling)
 
     def query_grads(c):
         parts = [dot(keyst[2 * c + h], dsall[2 * c + h]) for h in range(2)]
@@ -464,12 +470,10 @@
         gqf[...] = own_queries + gqsib[...].astype(F32)
         gqb[...] = gqf[...].astype(BF16)
 
-    between = [[functools.partial(block_sums, t) for t in range(1, min(blocks, 3))]]
-    between += [[functools.partial(block_sums, t)] for t in range(3, blocks)]
-    while len(between) < 3:
-        between.append([])
-    between[1] += [sibling_weight_grads]
-    between[2] += [sibling_query_grads, own_weight_grads]
+    between = [
+        [functools.partial(block_sums, t) for t in range(1, blocks)] + [sibling_weight_grads],
+        [sibling_query_grads, own_weight_grads], [own_query_grads],
+    ]
     block_sums(0)
     ring_step(0)
     for t in range(1, blocks):
@@ -478,24 +482,8 @@
         ring_step(t)
     for item in sum(between, []):
         item()
-    own_query_grads()
     gw_scatter.pass_on()
     gq_scatter.begin()
-
-    own_rows = pl.ds(pl.multiple_of(core * half, half), half)
-
-    @pl.when(core == 1)
-    def _():
-        for j in range(SUBS):
-            ring_copy(blocks - 1, j).wait_recv()
-            if j == SUBS // 2 - 1:
-                half_copy(rrecv.at[blocks - 1, pl.ds(0, half)]).start()
-        tot[half:, :] = rrecv[blocks - 1, half:, :].astype(F32)
-
-    half_copy(hsend).wait_recv()
-    ybuf[y] = (tot[own_rows, :] + hsib[...].astype(F32)).astype(BF16)
-
-    yhalf = half // 2
 
     def y_copy(slot, j, send, device):
         rows = pl.ds(j * yhalf, yhalf)
@@ -503,14 +491,39 @@
             ybuf.at[slot, rows], ybuf.at[slot, rows], y_s.at[send], y_r.at[2 * slot + j], device
         )
 
+    def last_pieces(j):
+        for k in range(j * SUBS // 4, (j + 1) * SUBS // 4):
+            ring_copy(blocks - 1, k).wait_recv()
+
+    @pl.when(core == 1)
+    def _():
+        for j in range(2):
+            last_pieces(j)
+            half_copy(rrecv.at[blocks - 1, pl.ds(j * yhalf, yhalf)], j).start()
+
     for j in range(2):
-        for k, device in enumerate(y_devices):
-            start(y_copy(y, (j + k) % 2, 2 * k + j, device))
+        @pl.when(core == 1)
+        def _():
+            last_pieces(2 + j)
+            rows = slice(half + j * yhalf, half + (j + 1) * yhalf)
+            tot[rows, :] = rrecv[blocks - 1, rows, :].astype(F32)
+
+        rows = slice(j * yhalf, (j + 1) * yhalf)
+        half_copy(hsend.at[pl.ds(j * yhalf, yhalf)], j).wait_recv()
+        mine_now = tot[pl.ds(pl.multiple_of(core * half + j * yhalf, yhalf), yhalf), :]
+        ybuf[y, rows, :] = (mine_now + hsib[rows, :].astype(F32)).astype(BF16)
+        if len(y_devices) == 2:
+            start(y_copy(y, j, j, y_devices[j]))
+        else:
+            start(y_copy(y, j, j, y_devices[0]))
+    if len(y_devices) == 2:
+        for j in range(2):
+            start(y_copy(y, j, 2 + j, y_devices[1 - j]))
 
     part = gw_scatter.finish(gwf[:, x])
     gwzf[...] = part
     gwzb[...] = part.astype(BF16)
-    for k, p in enumerate(z_peers):
+    for k, p in enumerate(reversed(z_peers)):
         start(remote(gwzb.at[p], gwzr.at[z], gwz_s.at[k], gwz_r.at[z], at_z(p)))
 
     gq_scatter.pass_on()
@@ -573,7 +586,8 @@
 
     for copy in sent:
         copy.wait_send()
-    half_copy(hsend).wait_send()
+    for j in range(2):
+        half_copy(hsend.at[pl.ds(j * yhalf, yhalf)], j).wait_send()
 
     @pl.when(core == 1)
     def _():
@@ -663,7 +677,7 @@
             dma((SUBS * blocks,)), dma((SUBS * blocks,)),
             dma((1,)), dma((1,)), dma((1,)), dma((1,)),
             dma((6,)), dma((6,)), dma((6,)), dma((6,)), dma((nz,)), dma((nz,)),
-            dma((1,)), dma((1,)), dma((6,)), dma((2 * nyh,)),
+            dma((2,)), dma((2,)), dma((6,)), dma((2 * nyh,)),
             dma((1,)), dma((CORES,)), dma((1,)), dma((1,)),
         ]
         out_shape = (

time: 62.6 us -> 62.4 us (level)
  no operation moved by 1% of the time
where the time goes in v5:
time: 62.4 us; the launch traced here: 62.2 us
  Pallas kernels  61.6 us (99%)
  between operations  0.64 us (1%)
    pallas_call x1, Pallas kernels, shards(): pl.pallas_call(functools.partial(kernel, nz, nyh, tok), out_shape=out_sha...  59.9 us
    pallas_call x1, Pallas kernels, shards(): pl.pallas_call(hand_over, out_shape=out_shape, in_specs=[vmem] * 6, out_s...  1.68 us

profile of v5, /device:TPU:1, one launch (start us, length us, event | category | flops | bytes accessed | tf_op | source)
XLA Modules:
  0.0 62.2 jit_solution(13694403296579008617)
XLA Ops:
  0.6 59.9 %shard_map.136 = (bf16[1,128,256]{2,1,0:T(8,128)(2,1)}, bf16[1,128,128]{2,1,0:T(8,128)(2,1)}, bf16[1,128,512]{2,1,0:T(8,128)(2,1)}, bf16[1,64,128]{2,1,0:T(8,128...) custom-call(bf16[1,128,512]{2,1,0:T(8,128)(2,1)} %lat_in.1, bf16[1,64,128]{2,1,0:T(8,128)(2,1)} %bitcast.2, ...), custom_call_target="tpu_custom_call" | custom-call | tf_op jit(solution)/shard_map/pallas_call | solution.py:691
  60.5 1.7 %shard_map.137 = (bf16[1,128,256]{2,1,0:T(8,128)(2,1)}, bf16[1,128,128]{2,1,0:T(8,128)(2,1)}, bf16[1,128,512]{2,1,0:T(8,128)(2,1)}, bf16[1,64,128]{2,1,0:T(8,128...) custom-call(bf16[1,128,256]{2,1,0:T(8,128)(2,1)} %get-tuple-element.18.refs_0_, ...), custom_call_target="tpu_custom_call" | custom-call | tf_op jit(solution)/shard_map/pallas_call | solution.py:701
